TPU v7x, 32 devices: a whole 2x2x4 slice. The times are simulated.
32 devices in a mesh: shard: 8 (over z, y), dp: 4 (over x, core).
Axes of the slice: x: 2, y: 2, z: 4, core: 2. Of those that a mesh axis runs over, the one named last changes fastest.
Arguments:
- cold_table: bfloat16 [16384, 256], P('shard'), may hold values from -6 to 6
- cold_accum: float32 [16384], P('shard'), may hold values from 0.005 to 0.5
- dither_bits: int32 [16384, 256], P('shard'), may hold values from 0 to 65280
- hot_table: float32 [1024, 256], replicated, may hold values from -6 to 6
- hot_accum: float32 [1024], replicated, may hold values from 1 to 100
- w_flat: bfloat16 [4096, 512], replicated, may hold values from -0.09375 to 0.09375
- w_inter: bfloat16 [256, 512], replicated, may hold values from -0.09375 to 0.09375
- hidden_bias: float32 [512], replicated, may hold values from -1 to 1
- w_out: float32 [512], replicated, may hold values from -0.25 to 0.25
- targets: float32 [16384], P(('shard', 'dp')), may hold values from 0 to 1
- hot_ids: int32 [16384, 8], P(('shard', 'dp')), may hold values from 0 to 1023
- cold_slots: int32 [16384, 8], P(('shard', 'dp')), may hold values from 0 to 2047, as said below
- requests: int32 [512, 256], P(('shard', 'dp')), may hold values from 0 to 2047, as said below
- counts: int32 [64, 8], P(('shard', 'dp')), may hold values from 1 to 256, as said below
Outputs:
- cold_out: bfloat16 [16384, 256], P('shard')
- cold_accum_out: float32 [16384], P('shard')
- hot_out: float32 [1024, 256], replicated
- hot_accum_out: float32 [1024], replicated
Inputs may be any that keep to these rules, and one draw needn't show every extreme that they name: `requests`: in each row of 256 entries (one device, micro-batch and shard) the entries name distinct rows of that shard's 2048; only the first counts-many are live, the rest name arbitrary rows. `counts`: in every draw, each device has in each micro-batch a shard with exactly 256 live slots. `cold_slots`: index into its device's request rows of that micro-batch, shard * 256 + slot; always a live slot, and every live slot is named by some lookup.
All inputs are finite; a program needn't handle non-finite values.
Results may differ from a plain program's by a relative error of at most 0.001.
The roundings to bfloat16 on the way count: a program that leaves them out, or rounds other values in their place, can miss the bound.
Values may be sent and summed in bfloat16 or wider, within the bound.
A program may use at most 128 MiB of HBM per device.

v0:
```python
import jax
import jax.numpy as jnp
from jax import lax
from jax.sharding import PartitionSpec as P

MB = 2
BATCH = 256


learn_rate = 0.3


def backprop(stacked, targets, w_flat, w_inter, hidden_bias, w_out):
    row_count, feature_count, row_width = stacked.shape
    flattened = stacked.reshape(row_count, feature_count * row_width)
    pair_dots = (
        jnp.einsum("sfe,sge->sfg", stacked, stacked, preferred_element_type=jnp.float32)
        * row_width ** (-0.5)
    ).astype(jnp.bfloat16)
    pre_act = jnp.dot(flattened, w_flat, preferred_element_type=jnp.float32)
    pre_act = pre_act + jnp.dot(
        pair_dots.reshape(row_count, feature_count * feature_count),
        w_inter,
        preferred_element_type=jnp.float32,
    )
    pre_act = pre_act + hidden_bias
    gated = jax.nn.sigmoid(pre_act)
    logits = jnp.sum(pre_act * gated * w_out, axis=-1)
    residual = jax.nn.sigmoid(logits) - targets
    slopes = (residual[:, None] * w_out * gated * (1.0 + pre_act * (1.0 - gated))).astype(
        jnp.bfloat16
    )
    back_flat = jnp.dot(slopes, w_flat.T, preferred_element_type=jnp.float32)
    back_pairs = jnp.dot(slopes, w_inter.T, preferred_element_type=jnp.float32).reshape(
        row_count, feature_count, feature_count
    )
    mirror = ((back_pairs + jnp.swapaxes(back_pairs, 1, 2)) * row_width ** (-0.5)).astype(
        jnp.bfloat16
    )
    return back_flat.reshape(row_count, feature_count, row_width) + jnp.einsum(
        "sfg,sge->sfe", mirror, stacked, preferred_element_type=jnp.float32
    )


def adagrad_rows(table_rows, accum, gradient):
    accum_new = accum + jnp.mean(gradient * gradient, axis=-1)
    updated = table_rows - learn_rate * gradient / jnp.sqrt(accum_new)[:, None]
    return (updated, accum_new)


def requantize(updated, bits, touched):
    grid_step = jnp.max(jnp.abs(updated), axis=-1, keepdims=True) / 8.0
    dither = bits.astype(jnp.float32) * (1.0 / 65280.0) - 0.5
    return jnp.where(touched[:, None], updated + grid_step * dither, updated).astype(jnp.bfloat16)


def on_device(
    cold_table,
    cold_accum,
    dither_bits,
    hot_table,
    hot_accum,
    w_flat,
    w_inter,
    hidden_bias,
    w_out,
    targets,
    hot_ids,
    cold_slots,
    requests,
    counts,
):
    shards = lax.axis_size("shard")
    capacity = requests.shape[1]
    row_count = cold_table.shape[0]
    row_width = cold_table.shape[1]
    hot_count = hot_table.shape[0]
    cold_feats = cold_slots.shape[1]
    hot_grad = jnp.zeros((hot_count, row_width), jnp.float32)
    asked_rows = (
        requests.reshape(MB, shards, capacity).transpose(1, 0, 2).reshape(shards, MB * capacity)
    )
    requested = lax.all_to_all(asked_rows, "shard", split_axis=0, concat_axis=0, tiled=True)
    fetched_all = lax.all_to_all(
        cold_table[requested], "shard", split_axis=0, concat_axis=0, tiled=True
    )
    slot_list = []
    for micro_index in range(MB):
        fetched_rows = fetched_all[:, micro_index * capacity : (micro_index + 1) * capacity]
        first = micro_index * BATCH
        slot_part = cold_slots[first : first + BATCH]
        hot_part = hot_ids[first : first + BATCH]
        cold_vectors = fetched_rows.reshape(shards * capacity, row_width)[slot_part]
        stacked = jnp.concatenate([cold_vectors, hot_table[hot_part].astype(jnp.bfloat16)], axis=1)
        gradients = backprop(
            stacked, targets[first : first + BATCH], w_flat, w_inter, hidden_bias, w_out
        )
        slot_grad = jax.ops.segment_sum(
            gradients[:, :cold_feats].reshape(-1, row_width),
            slot_part.reshape(-1),
            num_segments=shards * capacity,
        )
        hot_term = jax.ops.segment_sum(
            gradients[:, cold_feats:].reshape(-1, row_width),
            hot_part.reshape(-1),
            num_segments=hot_count,
        )
        slot_grad, hot_term = (slot_grad.reshape(shards, capacity, row_width), hot_term)
        hot_grad = hot_grad + hot_term
        slot_list.append(slot_grad)
    joined_grad = jnp.concatenate(slot_list, axis=1)
    owner_grad, count_in = (
        lax.all_to_all(
            joined_grad.astype(jnp.bfloat16), "shard", split_axis=0, concat_axis=0, tiled=True
        ).astype(joined_grad.dtype),
        lax.all_to_all(counts.T, "shard", split_axis=0, concat_axis=0, tiled=True),
    )
    cold_grad = jax.ops.segment_sum(
        owner_grad.reshape(-1, row_width), requested.reshape(-1), num_segments=row_count
    )
    live_mask = (
        jnp.arange(capacity, dtype=jnp.int32)[None, None, :] < count_in[:, :, None]
    ).astype(jnp.float32)
    touched = jax.ops.segment_sum(
        live_mask.reshape(-1), requested.reshape(-1), num_segments=row_count
    )
    summed_grad, summed_hits = (
        lax.psum(cold_grad.astype(jnp.bfloat16), "dp").astype(jnp.float32),
        lax.psum(touched.astype(jnp.bfloat16), "dp").astype(jnp.float32),
    )
    averaged = summed_grad / jnp.maximum(summed_hits, 1.0)[:, None]
    updated, cold_accum_out = adagrad_rows(cold_table.astype(jnp.float32), cold_accum, averaged)
    cold_out = requantize(updated, dither_bits, summed_hits > 0.5)
    total_hot = lax.psum(hot_grad, ("shard", "dp"))
    hot_out, hot_accum_out = adagrad_rows(hot_table, hot_accum, total_hot)
    return (cold_out, cold_accum_out, hot_out, hot_accum_out)


def solution(mesh):
    return jax.shard_map(
        on_device,
        mesh=mesh,
        in_specs=(
            P("shard", None),
            P("shard"),
            P("shard", None),
            P(),
            P(),
            P(),
            P(),
            P(),
            P(),
            P(("shard", "dp")),
            P(("shard", "dp"), None),
            P(("shard", "dp"), None),
            P(("shard", "dp"), None),
            P(("shard", "dp"), None),
        ),
        out_specs=(P("shard", None), P("shard"), P(), P()),
        check_vma=False,
    )
```

profile of v0, /device:TPU:0, one launch (start us, length us, event | category | flops | bytes accessed | tf_op | source)
XLA Modules:
  0.0 450.8 jit_solution(6460371465617464452)
XLA Ops:
  8.8 13.7 %all_to_all.32 = s32[8,1,512]{2,1,0:T(1,128)S(1)} all-to-all(s32[8,1,512]{2,1,0:T(1,128)S(1)} %all_to_all.27), channel_id=1, replica_groups=mesh['shard'=8,'dp'=4] {'shard'}, dimensions={0} | all-to-all | bytes 32768 | tf_op jit(solution)/shard_map/all_to_all | solution.py:83
  22.5 17.3 %gather_fusion = bf16[4096,256]{1,0:T(8,128)(2,1)} fusion(bf16[2048,256]{1,0:T(8,128)(2,1)} %param.14, s32[4096]{0:T(1024)S(1)} %broadcast_clamp_fusion), kind=kCustom, calls=%fused_computation | custom fusion | bytes 4210688 | tf_op jit(solution)/shard_map/gather | solution.py:85
  39.8 3.7 all-to-all-start.2
  51.0 1.3 fusion.26
  56.1 8.5 %gather_fusion.4 = bf16[2048,256]{1,0:T(8,128)(2,1)} fusion(f32[1024,256]{1,0:T(8,128)S(1)} %copy-done.2, s32[2048]{0:T(1024)S(1)} %broadcast_clamp_fusion.1), kind=kCustom, calls=%fused_computation.4 | custom fusion | bytes 2105344 | tf_op jit(solution)/shard_map/gather | solution.py:94
  64.6 8.5 %gather_fusion.2 = bf16[2048,256]{1,0:T(8,128)(2,1)} fusion(f32[1024,256]{1,0:T(8,128)S(1)} %copy-done.2, s32[2048]{0:T(1024)S(1)} %broadcast_clamp_fusion.2), kind=kCustom, calls=%fused_computation.2 | custom fusion | bytes 2105344 | tf_op jit(solution)/shard_map/gather | solution.py:94
  73.1 17.4 %all-to-all-done.2 = bf16[8,512,256]{2,1,0:T(8,128)(2,1)S(1)} async-done(((bf16[8,512,256]{2,1,0:T(8,128)(2,1)}), bf16[8,512,256]{2,1,0:T(8,128)(2,1)S(1)}, u32[]{:S(2)}, u32[]{:S(2)}) %all-to-all-start.2) | async-done | bytes 2097184 | tf_op jit(solution)/shard_map/all_to_all | solution.py:84
  90.5 1.3 copy-done.11
  91.9 3.9 all-to-all-start.1
  95.8 1.7 fusion.25
  97.5 9.1 %gather_fusion.3 = bf16[2048,256]{1,0:T(8,128)(2,1)} fusion(bf16[2048,256]{1,0:T(8,128)(2,1)S(1)} %bitcast.87, s32[2048]{0:T(1024)S(1)} %broadcast_clamp_fusion.3), kind=kCustom, calls=%fused_computation.3 | custom fusion | bytes 2105344 | tf_op jit(solution)/shard_map/gather | solution.py:93
  106.6 4.4 fusion.21
  110.9 1.5 pad_maximum_fusion.1
  112.4 9.2 %gather_fusion.1 = bf16[2048,256]{1,0:T(8,128)(2,1)} fusion(bf16[2048,256]{1,0:T(8,128)(2,1)S(1)} %bitcast.86, s32[2048]{0:T(1024)S(1)} %broadcast_clamp_fusion.4), kind=kCustom, calls=%fused_computation.1 | custom fusion | bytes 2105344 | tf_op jit(solution)/shard_map/gather | solution.py:93
  121.7 3.6 fusion.22
  125.3 1.5 pad_maximum_fusion
  126.8 3.2 copy.70
  130.9 3.9 copy.79
  134.8 3.2 copy.64
  139.0 2.7 copy.77
  141.8 2.8 fusion.31
  144.6 1.2 fusion.28
  147.6 3.2 fusion.32
  151.1 3.3 fusion.29
  154.7 1.9 copy.72
  156.6 1.9 copy.66
  158.5 4.3 copy.80
  162.8 2.9 bitcast_add_fusion
  165.7 13.6 %scatter_custom_fusion.2 = f32[2048,256]{1,0:T(8,128)} fusion(s32[2048]{0:T(1024)} %reshape.202, f32[256,16,256]{2,1,0:T(8,128)} %bitcast_add_fusion, f32[]{:T(128)} %constant.13.clone.1), kind=kCustom, calls=%fused_computation.22 | custom fusion | flops 524288 | bytes 4194816 | tf_op jit(solution)/shard_map/scatter-add | solution.py:98
  179.2 2.7 convert.11
  181.9 4.0 copy.78
  185.9 2.9 bitcast_add_fusion.1
  188.9 12.6 %scatter_custom_fusion.1 = f32[2048,256]{1,0:T(8,128)S(1)} fusion(s32[2048]{0:T(1024)} %reshape.194, f32[256,16,256]{2,1,0:T(8,128)} %bitcast_add_fusion.1, f32[]{:T(128)} %constant.13.clone.1), kind=kCustom, calls=%fused_computation.24 | custom fusion | flops 524288 | bytes 4194816 | tf_op jit(solution)/shard_map/scatter-add | solution.py:98
  202.7 1.5 pad_maximum_fusion.2
  204.2 6.0 %all-to-all-start.3 = ((bf16[8,512,256]{2,1,0:T(8,128)(2,1)}), bf16[8,512,256]{2,1,0:T(8,128)(2,1)S(1)}, u32[]{:S(2)}, u32[]{:S(2)}) async-start(bf16[8,512,256]{2,1,0:T(8,128)(2,1)} %pad_maximum_fusion.2), calls=%async_computation.3 | async-start | bytes 4194304 | tf_op jit(solution)/shard_map/all_to_all | solution.py:113
  210.8 13.3 %scatter_custom_fusion.5 = f32[1024,256]{1,0:T(8,128)} fusion(s32[2048]{0:T(1024)S(1)} %reshape.226, f32[256,16,256]{2,1,0:T(8,128)} %bitcast_add_fusion, f32[]{:T(128)} %constant.13.clone.1), kind=kCustom, calls=%fused_computation.18 | custom fusion | flops 524288 | bytes 3146240 | tf_op jit(solution)/shard_map/scatter-add | solution.py:103
  224.2 13.1 %scatter_custom_fusion.4 = f32[1024,256]{1,0:T(8,128)} fusion(s32[2048]{0:T(1024)S(1)} %reshape.218, f32[256,16,256]{2,1,0:T(8,128)} %bitcast_add_fusion.1, f32[]{:T(128)} %constant.13.clone.1), kind=kCustom, calls=%fused_computation.20 | custom fusion | flops 524288 | bytes 3146240 | tf_op jit(solution)/shard_map/scatter-add | solution.py:103
  237.3 2.6 add.129
  240.8 22.1 %scatter_custom_fusion = f32[2048]{0:T(1024)S(1)} fusion(s32[4096]{0:T(1024)S(1)} %bitcast.114, f32[4096]{0:T(1024)S(1)} %bitcast.119, f32[]{:T(128)} %constant.13.clone.1), kind=kCustom, calls=%fused_computation.77 | custom fusion | flops 4096 | bytes 8196 | tf_op jit(solution)/shard_map/scatter-add | solution.py:124
  262.8 6.0 %psum.21 = bf16[2048]{0:T(1024)(128)(2,1)S(1)} all-reduce(bf16[2048]{0:T(1024)(128)(2,1)S(1)} %convert_element_type.56), channel_id=1, replica_groups=mesh['shard'=8,'dp'=4] {'dp'}, use_global_device_ids=true, to_apply=%region_1.0 | all-reduce | flops 2048 | bytes 8192 | tf_op jit(solution)/shard_map/psum | solution.py:129
  268.8 103.8 %all-reduce.5.cloned.1.call-done = f32[1024,256]{1,0:T(8,128)} async-done(((f32[1024,256]{1,0:T(8,128)}), f32[1024,256]{1,0:T(8,128)}) %all-reduce.5.cloned.1.call-update) | async-done | bytes 1048592 | tf_op jit(solution)/shard_map/psum | solution.py:134
  372.6 1.4 multiply_reduce_fusion.1
  374.1 24.1 %scatter_custom_fusion.3 = f32[2048,256]{1,0:T(8,128)} fusion(s32[4096]{0:T(1024)S(1)} %bitcast.115, bf16[4096,256]{1,0:T(8,128)(2,1)S(1)} %bitcast.102, f32[]{:T(128)} %constant.13.clone.1), kind=kCustom, calls=%fused_computation.13 | custom fusion | flops 2097152 | bytes 4194308 | tf_op jit(solution)/shard_map/scatter-add | solution.py:118
  398.1 2.8 convert_element_type.67
  402.7 33.9 %all-reduce.3.cloned.1.call-done = bf16[2048,256]{1,0:T(8,128)(2,1)} async-done(((bf16[2048,256]{1,0:T(8,128)(2,1)}), bf16[2048,256]{1,0:T(8,128)(2,1)}) %all-reduce.3.cloned.1.call-update) | async-done | bytes 1048592 | tf_op jit(solution)/shard_map/psum | solution.py:128
  436.6 1.9 multiply_reduce_fusion
  439.1 2.2 abs_reduce_fusion
  441.4 1.5 fusion.2
  (109 shorter events, 21.3 us)
Async XLA Ops:
  8.0 137.9 %copy-start = (bf16[256,512]{1,0:T(8,128)(2,1)S(1)}, bf16[256,512]{1,0:T(8,128)(2,1)}, u32[]{:S(2)}) copy-start(bf16[256,512]{1,0:T(8,128)(2,1)} %param.20) | copy-start | bytes 786436
  39.8 3.8 copy-start.28
  39.8 4.4 copy-start.22
  39.8 16.3 %copy-start.2 = (f32[1024,256]{1,0:T(8,128)S(1)}, f32[1024,256]{1,0:T(8,128)}, u32[]{:S(2)}) copy-start(f32[1024,256]{1,0:T(8,128)} %param.17) | copy-start | bytes 3145732
  39.8 50.8 %all-to-all-start.2 = ((bf16[8,512,256]{2,1,0:T(8,128)(2,1)}), bf16[8,512,256]{2,1,0:T(8,128)(2,1)S(1)}, u32[]{:S(2)}, u32[]{:S(2)}) async-start(bf16[8,512,256]{2,1,0:T(8,128)(2,1)} %bitcast.105), calls=%async_computation.2 | async-start | bytes 4194304 | tf_op jit(solution)/shard_map/all_to_all | solution.py:84
  56.1 8.5 %copy-start.19 = (s32[2048]{0:T(1024)S(1)}, s32[2048]{0:T(1024)}, u32[]{:S(2)}) copy-start(s32[2048]{0:T(1024)} %reshape.162) | copy-start | bytes 24580
  64.6 8.5 %copy-start.17 = (s32[2048]{0:T(1024)S(1)}, s32[2048]{0:T(1024)}, u32[]{:S(2)}) copy-start(s32[2048]{0:T(1024)} %reshape.154) | copy-start | bytes 24580
  64.6 8.5 %copy-start.18 = (s32[2048]{0:T(1024)S(1)}, s32[2048]{0:T(1024)}, u32[]{:S(2)}) copy-start(s32[2048]{0:T(1024)} %reshape.170) | copy-start | bytes 24580
  90.5 1.3 copy-start.11
  91.9 112.3 %all-to-all-start.1 = ((s32[8,1,2]{2,1,0:T(1,128)}), s32[8,1,2]{2,1,0:T(1,128)}, u32[]{:S(2)}, u32[]{:S(2)}) async-start(s32[8,1,2]{2,1,0:T(1,128)} %copy.58), calls=%async_computation.1 | async-start | bytes 8192 | tf_op jit(solution)/shard_map/all_to_all | solution.py:116
  106.6 4.4 copy-start.6
  106.6 4.4 copy-start.9
  112.4 9.2 %copy-start.5 = (bf16[2048,256]{1,0:T(8,128)(2,1)S(1)}, bf16[2048,256]{1,0:T(8,128)(2,1)}, u32[]{:S(2)}) copy-start(bf16[2048,256]{1,0:T(8,128)(2,1)} %gather_fusion.2) | copy-start | bytes 3145732
  121.7 3.6 copy-start.8
  139.0 2.8 copy-start.4
  144.6 1.3 copy-start.25
  144.6 1.5 copy-start.26
  146.2 0.7 copy-start.27
  158.5 4.3 copy-start.7
  158.5 4.3 copy-start.10
  158.5 4.3 copy-start.15
  181.9 4.0 copy-start.14
  201.5 1.2 copy-start.13
  204.2 6.1 %copy-start.21 = (s32[256,8]{0,1:T(8,128)S(1)}, s32[256,8]{0,1:T(8,128)}, u32[]{:S(2)}) copy-start(s32[256,8]{0,1:T(8,128)} %get-tuple-element.14) | copy-start | bytes 24580
  204.2 6.3 %copy-start.20 = (s32[256,8]{0,1:T(8,128)S(1)}, s32[256,8]{0,1:T(8,128)}, u32[]{:S(2)}) copy-start(s32[256,8]{0,1:T(8,128)} %get-tuple-element.17) | copy-start | bytes 24580
  204.2 169.8 %all-to-all-start.3 = ((bf16[8,512,256]{2,1,0:T(8,128)(2,1)}), bf16[8,512,256]{2,1,0:T(8,128)(2,1)S(1)}, u32[]{:S(2)}, u32[]{:S(2)}) async-start(bf16[8,512,256]{2,1,0:T(8,128)(2,1)} %pad_maximum_fusion.2), calls=%async_computation.3 | async-start | bytes 4194304 | tf_op jit(solution)/shard_map/all_to_all | solution.py:113
  210.3 162.4 %all-reduce.5.cloned.1.call-start = ((), (), s32[]{:S(2)}) async-start(), calls=%async_computation.5 | async-start | bytes 2097152 | tf_op jit(solution)/shard_map/psum | solution.py:134
  239.9 196.7 %all-reduce.3.cloned.1.call-start = ((), (), s32[]{:S(2)}) async-start(), calls=%async_computation.4 | async-start | bytes 2097152 | tf_op jit(solution)/shard_map/psum | solution.py:128
  398.1 2.8 copy-start.24
  398.1 3.4 copy-start.12
  401.5 37.0 %copy-start.23 = (f32[2048]{0:T(1024)S(1)}, f32[2048]{0:T(1024)}, u32[]{:S(2)}) copy-start(f32[2048]{0:T(1024)} %param.15) | copy-start | bytes 24580
  401.5 37.6 %copy-start.3 = (bf16[2048,256]{1,0:T(8,128)(2,1)S(1)}, bf16[2048,256]{1,0:T(8,128)(2,1)}, u32[]{:S(2)}) copy-start(bf16[2048,256]{1,0:T(8,128)(2,1)} %param.14) | copy-start | bytes 3145732
  439.1 2.2 copy-start.16
  441.4 1.5 copy-start.1
Sparse Core Ops, SparseCore 0:
  240.0 132.5 all-reduce.4
Sparse Core Ops, SparseCore 1:
  401.0 35.6 all-reduce.2
where the time goes:
time: 456 us; the launch traced here: 451 us
  waiting for transfers between devices  155 us (34%)
  other arithmetic  127 us (28%)
  local copies, waits for them, and re-layouts  93.1 us (20%)
  matrix products  25.7 us (6%)
  blocking collectives  19.6 us (4%)
  between operations  16.4 us (4%)
  starting transfers between devices  13.8 us (3%)
    psum x1, waiting for transfers between devices, on_device(): total_hot = lax.psum(hot_grad, ('shard', 'dp'))  104 us
    psum x1, waiting for transfers between devices, on_device(): lax.psum(cold_grad.astype(jnp.bfloat16), 'dp').astype(jnp.float32)  33.9 us
    scatter-add x2, other arithmetic, on_device(): jax.ops.segment_sum(gradients[:, cold_feats:].reshape(-1, row_width), hot...  26.4 us
    scatter-add x2, other arithmetic, on_device(): jax.ops.segment_sum(gradients[:, :cold_feats].reshape(-1, row_width), slo...  26.2 us
    scatter-add x1, other arithmetic, on_device(): jax.ops.segment_sum(owner_grad.reshape(-1, row_width), requested.reshape(...  24.1 us
    scatter-add x1, other arithmetic, on_device(): jax.ops.segment_sum(live_mask.reshape(-1), requested.reshape(-1), num_seg...  22.1 us
    gather x2, local copies, waits for them, and re-layouts, on_device(): cold_vectors = fetched_rows.reshape(shards * capacity, row_width)[slot_part]  18.2 us
    unnamed x63, local copies, waits for them, and re-layouts  17.7 us
  transfers between devices with their start and end apart: 5, of which 3 were waited for; matrix products, arithmetic and copies ran while one was open for 43% of the time, Pallas kernels for 0%

commit v1 on v0

v1 whole, which is shorter than its diff:
```python
import functools

import jax
import jax.numpy as jnp
from jax import lax
from jax.experimental import pallas as pl
from jax.experimental.pallas import tpu as pltpu
from jax.sharding import PartitionSpec as P

learn_rate = 0.3
BF = jnp.bfloat16
F32 = jnp.float32
VMEM_LIMIT = 52 * 1024 * 1024


def dot(a, b):
    return lax.dot_general(a, b, (((1,), (0,)), ((), ())), preferred_element_type=F32)


def dot_t(a, b):
    return lax.dot_general(a, b, (((1,), (1,)), ((), ())), preferred_element_type=F32)


def hot_one(rows, columns, ids, axis, first):
    spots = lax.broadcasted_iota(jnp.int32, (rows, columns), axis) + first
    return jnp.where(spots == ids, 1.0, 0.0)


def owner_gather_kernel(ids_ref, table_ref, rows_ref, hits_ref):
    rows = table_ref.shape[0]
    pick = hot_one(ids_ref.shape[0], rows, ids_ref[...], 1, 0)
    rows_ref[...] = dot(pick.astype(BF), table_ref[...]).astype(BF)

    @pl.when(pl.program_id(0) == 0)
    def _():
        hits_ref[...] = jnp.zeros_like(hits_ref)

    hits_ref[...] += jnp.sum(pick, axis=0, keepdims=True)


def owner_gather(ids, table):
    count, (rows, width) = ids.shape[0], table.shape
    tile = min(256, count)
    return pl.pallas_call(
        owner_gather_kernel,
        grid=(count // tile,),
        in_specs=[
            pl.BlockSpec((tile, 1), lambda i: (i, 0)),
            pl.BlockSpec((rows, width), lambda i: (0, 0)),
        ],
        out_specs=[
            pl.BlockSpec((tile, width), lambda i: (i, 0)),
            pl.BlockSpec((1, rows), lambda i: (0, 0)),
        ],
        out_shape=[
            jax.ShapeDtypeStruct((count, width), BF),
            jax.ShapeDtypeStruct((1, rows), F32),
        ],
        compiler_params=pltpu.CompilerParams(vmem_limit_bytes=VMEM_LIMIT),
        cost_estimate=pl.CostEstimate(
            flops=2 * count * rows * width,
            bytes_accessed=2 * (count + rows) * width,
            transcendentals=0,
        ),
    )(ids, table)


def owner_scatter_kernel(ids_ref, grad_ref, out_ref):
    tile = out_ref.shape[0]
    count = ids_ref.shape[1]
    pick = hot_one(tile, count, ids_ref[...], 0, pl.program_id(0) * tile)
    out_ref[...] = dot(pick.astype(BF), grad_ref[...]).astype(out_ref.dtype)


def owner_scatter(ids, grads, rows):
    count, width = grads.shape
    tile = min(256, rows)
    return pl.pallas_call(
        owner_scatter_kernel,
        grid=(rows // tile,),
        in_specs=[
            pl.BlockSpec((1, count), lambda i: (0, 0)),
            pl.BlockSpec((count, width), lambda i: (0, 0)),
        ],
        out_specs=pl.BlockSpec((tile, width), lambda i: (i, 0)),
        out_shape=jax.ShapeDtypeStruct((rows, width), BF),
        compiler_params=pltpu.CompilerParams(vmem_limit_bytes=VMEM_LIMIT),
        cost_estimate=pl.CostEstimate(
            flops=2 * count * rows * width,
            bytes_accessed=2 * (count + rows) * width,
            transcendentals=0,
        ),
    )(ids, grads)


def train_kernel(
    fetched_ref,
    cold_col_ref,
    cold_row_ref,
    hot_col_ref,
    hot_row_ref,
    hot_ref,
    w_flat_ref,
    w_inter_ref,
    w_turned_ref,
    bias_ref,
    w_out_ref,
    targets_ref,
    hot_before_ref,
    slot_grad_ref,
    hot_grad_ref,
    x_ref,
    pairs_ref,
    grad_ref,
    high_ref,
    low_ref,
):
    feats, samples, width = x_ref.shape
    cold = cold_col_ref.shape[0] // samples
    slots = fetched_ref.shape[0]
    hot_count = hot_ref.shape[0]
    scale = width ** (-0.5)
    group = 16
    side = feats * group
    square = feats * feats

    def fill_cold(f, carry):
        ids = cold_col_ref[pl.ds(pl.multiple_of(f * samples, samples), samples), :]
        pick = hot_one(samples, slots, ids, 1, 0).astype(BF)
        x_ref[f] = dot(pick, fetched_ref[...]).astype(BF)
        return carry

    lax.fori_loop(0, cold, fill_cold, 0)

    def fill_hot(f, carry):
        ids = hot_col_ref[pl.ds(pl.multiple_of(f * samples, samples), samples), :]
        pick = hot_one(samples, hot_count, ids, 1, 0).astype(BF)
        x_ref[f + cold] = dot(pick, hot_ref[...]).astype(BF)
        return carry

    lax.fori_loop(0, feats - cold, fill_hot, 0)

    def grid_of(shape, axis):
        return lax.broadcasted_iota(jnp.int32, shape, axis)

    same_sample = grid_of((side, side), 0) % group == grid_of((side, side), 1) % group
    same_feature = grid_of((side, square), 0) // group == grid_of((side, square), 1) // feats
    spread = jnp.where(
        grid_of((side, square), 0) // group == grid_of((side, square), 1) % feats, 1.0, 0.0
    ).astype(BF)

    def pair_step(b, carry):
        at = pl.ds(pl.multiple_of(b * group, group), group)
        part = x_ref[:, at, :].reshape(side, width)
        grams = dot_t(part, part) * scale
        grams = jnp.where(same_sample, grams, 0.0).astype(BF)
        wide = jnp.where(same_feature, dot(grams, spread), 0.0)
        pairs_ref[at, :] = jnp.sum(wide.reshape(feats, group, square), axis=0).astype(BF)
        return carry

    lax.fori_loop(0, samples // group, pair_step, 0, unroll=2)

    pre = dot(pairs_ref[...], w_inter_ref[...]) + bias_ref[...]
    for f in range(feats):
        pre = pre + dot(x_ref[f], w_flat_ref[f * width : (f + 1) * width, :])
    gated = jax.nn.sigmoid(pre)
    w_out = w_out_ref[...]
    logits = jnp.sum(pre * gated * w_out, axis=-1, keepdims=True)
    residual = jax.nn.sigmoid(logits) - targets_ref[...]
    slopes = (residual * w_out * gated * (1.0 + pre * (1.0 - gated))).astype(BF)

    mirror = (dot_t(slopes, w_inter_ref[...]) + dot_t(slopes, w_turned_ref[...])) * scale
    pairs_ref[...] = mirror.astype(BF)

    def mirror_step(b, carry):
        at = pl.ds(pl.multiple_of(b * group, group), group)
        part = x_ref[:, at, :].reshape(side, width)
        one = pairs_ref[at, :].astype(F32)
        many = jnp.broadcast_to(one[None], (feats, group, square)).reshape(side, square)
        many = jnp.where(same_feature, many, 0.0).astype(BF)
        turned = jnp.where(same_sample, dot_t(many, spread), 0.0).astype(BF)
        grad_ref[:, at, :] = dot(turned, part).reshape(feats, group, width)
        return carry

    lax.fori_loop(0, samples // group, mirror_step, 0, unroll=2)

    for f in range(feats):
        back = dot_t(slopes, w_flat_ref[f * width : (f + 1) * width, :]) + grad_ref[f]
        high = back.astype(BF)
        high_ref[f * samples : (f + 1) * samples, :] = high
        if f >= cold:
            low_ref[(f - cold) * samples : (f - cold + 1) * samples, :] = (
                back - high.astype(F32)
            ).astype(BF)

    tile = 256
    edge = cold * samples

    def spill_cold(c, carry):
        first = pl.multiple_of(c * tile, tile)
        pick = hot_one(tile, edge, cold_row_ref[...], 0, first).astype(BF)
        slot_grad_ref[pl.ds(first, tile), :] = dot(pick, high_ref[:edge, :]).astype(BF)
        return carry

    lax.fori_loop(0, slots // tile, spill_cold, 0)

    def spill_hot(c, carry):
        first = pl.multiple_of(c * tile, tile)
        pick = hot_one(tile, hot_row_ref.shape[1], hot_row_ref[...], 0, first).astype(BF)
        total = dot(pick, high_ref[edge:, :]) + dot(pick, low_ref[...])
        at = pl.ds(first, tile)
        hot_grad_ref[at, :] = hot_before_ref[at, :] + total
        return carry

    lax.fori_loop(0, hot_count // tile, spill_hot, 0)


def train(*operands):
    fetched, cold_col, _, hot_col, _, hot_rows, w_flat = operands[:7]
    samples = operands[11].shape[0]
    slots, width = fetched.shape
    feats = (cold_col.shape[0] + hot_col.shape[0]) // samples
    hidden = w_flat.shape[1]
    return pl.pallas_call(
        train_kernel,
        in_specs=[pl.BlockSpec(memory_space=pltpu.VMEM)] * len(operands),
        out_specs=[pl.BlockSpec(memory_space=pltpu.VMEM)] * 2,
        out_shape=[
            jax.ShapeDtypeStruct((slots, width), BF),
            jax.ShapeDtypeStruct(hot_rows.shape, F32),
        ],
        scratch_shapes=[
            pltpu.VMEM((feats, samples, width), BF),
            pltpu.VMEM((samples, feats * feats), BF),
            pltpu.VMEM((feats, samples, width), F32),
            pltpu.VMEM((feats * samples, width), BF),
            pltpu.VMEM((hot_col.shape[0], width), BF),
        ],
        compiler_params=pltpu.CompilerParams(vmem_limit_bytes=VMEM_LIMIT),
        cost_estimate=pl.CostEstimate(
            flops=4 * samples * feats * width * (hidden + slots + hot_rows.shape[0]),
            bytes_accessed=12 * 1024 * 1024,
            transcendentals=samples * hidden,
        ),
    )(*operands)


def cold_update_kernel(parts_ref, hits_ref, table_ref, accum_ref, bits_ref, out_ref, accum_out_ref):
    grad = parts_ref[0].astype(F32)
    for d in range(1, parts_ref.shape[0]):
        grad = grad + parts_ref[d].astype(F32)
    hits = hits_ref[...]
    averaged = grad / jnp.maximum(hits, 1.0)
    accum = accum_ref[...] + jnp.mean(averaged * averaged, axis=-1, keepdims=True)
    updated = table_ref[...].astype(F32) - learn_rate * averaged / jnp.sqrt(accum)
    step = jnp.max(jnp.abs(updated), axis=-1, keepdims=True) / 8.0
    dither = bits_ref[...].astype(F32) * (1.0 / 65280.0) - 0.5
    out_ref[...] = jnp.where(hits > 0.5, updated + step * dither, updated).astype(BF)
    accum_out_ref[...] = accum


def cold_update(parts, hits, table, accum, bits):
    return pl.pallas_call(
        cold_update_kernel,
        in_specs=[pl.BlockSpec(memory_space=pltpu.VMEM)] * 5,
        out_specs=[pl.BlockSpec(memory_space=pltpu.VMEM)] * 2,
        out_shape=[
            jax.ShapeDtypeStruct(table.shape, BF),
            jax.ShapeDtypeStruct(accum.shape, F32),
        ],
        compiler_params=pltpu.CompilerParams(vmem_limit_bytes=VMEM_LIMIT),
    )(parts, hits, table, accum, bits)


def swap(block, axis):
    return lax.all_to_all(block, axis, split_axis=0, concat_axis=0, tiled=True)


def on_device(
    cold_table,
    cold_accum,
    dither_bits,
    hot_table,
    hot_accum,
    w_flat,
    w_inter,
    hidden_bias,
    w_out,
    targets,
    hot_ids,
    cold_slots,
    requests,
    counts,
):
    shards = lax.axis_size("shard")
    copies = lax.axis_size("dp")
    micros = counts.shape[0]
    capacity = requests.shape[1]
    row_count, width = cold_table.shape
    hot_count = hot_table.shape[0]
    samples = targets.shape[0] // micros
    feats = cold_slots.shape[1] + hot_ids.shape[1]

    asked = requests.reshape(micros, shards, capacity)
    live = jnp.arange(capacity, dtype=jnp.int32)[None, None, :] < counts[:, :, None]
    asked = jnp.where(live, asked, -1).transpose(1, 0, 2)
    requested = swap(asked.reshape(shards, micros * capacity), "shard")
    requested = requested.reshape(shards, micros, capacity)

    fetched = []
    hits = jnp.zeros((1, row_count), F32)
    for m in range(micros):
        rows, part_hits = owner_gather(requested[:, m].reshape(-1, 1), cold_table)
        hits = hits + part_hits
        fetched.append(
            swap(rows.reshape(shards, capacity, width), "shard").reshape(shards * capacity, width)
        )
    hits = lax.psum(hits.reshape(row_count), "dp")

    turned = w_inter.reshape(feats, feats, -1).transpose(1, 0, 2).reshape(w_inter.shape)
    hot_rows = hot_table.astype(BF)
    cold_ids = cold_slots.reshape(micros, samples, -1).transpose(0, 2, 1).reshape(micros, -1)
    hot_names = hot_ids.reshape(micros, samples, -1).transpose(0, 2, 1).reshape(micros, -1)
    hot_grad = jnp.zeros(hot_table.shape, F32)
    owner_parts = []
    for m in range(micros):
        slot_grad, hot_grad = train(
            fetched[m],
            cold_ids[m].reshape(-1, 1),
            cold_ids[m].reshape(1, -1),
            hot_names[m].reshape(-1, 1),
            hot_names[m].reshape(1, -1),
            hot_rows,
            w_flat,
            w_inter,
            turned,
            hidden_bias.reshape(1, -1),
            w_out.reshape(1, -1),
            targets[m * samples : (m + 1) * samples].reshape(-1, 1),
            hot_grad,
        )
        owner_parts.append(swap(slot_grad.reshape(shards, capacity, width), "shard"))
    owner_grad = jnp.concatenate([part.reshape(-1, width) for part in owner_parts], axis=0)
    owner_ids = requested.transpose(1, 0, 2).reshape(1, -1)
    cold_grad = owner_scatter(owner_ids, owner_grad, row_count)

    share = row_count // copies
    parts = swap(cold_grad.reshape(copies, share, width), "dp")
    first = lax.axis_index("dp") * share
    cold_out, cold_accum_out = cold_update(
        parts,
        lax.dynamic_slice_in_dim(hits, first, share).reshape(-1, 1),
        lax.dynamic_slice_in_dim(cold_table, first, share),
        lax.dynamic_slice_in_dim(cold_accum, first, share).reshape(-1, 1),
        lax.dynamic_slice_in_dim(dither_bits, first, share),
    )
    cold_out = lax.all_gather(cold_out, "dp", tiled=True)
    cold_accum_out = lax.all_gather(cold_accum_out.reshape(-1), "dp", tiled=True)

    hot_part = jnp.sum(swap(hot_grad.reshape(copies, hot_count // copies, width), "dp"), axis=0)
    hot_part = hot_part.reshape(shards, -1, width)
    hot_part = jnp.sum(swap(hot_part, "shard"), axis=0)
    hot_total = lax.all_gather(hot_part, "shard", tiled=True)
    hot_total = lax.all_gather(hot_total, "dp", tiled=True)
    hot_accum_out = hot_accum + jnp.mean(hot_total * hot_total, axis=-1)
    hot_out = hot_table - learn_rate * hot_total / jnp.sqrt(hot_accum_out)[:, None]
    return (cold_out, cold_accum_out, hot_out, hot_accum_out)


def solution(mesh):
    return jax.shard_map(
        on_device,
        mesh=mesh,
        in_specs=(
            P("shard", None),
            P("shard"),
            P("shard", None),
            P(),
            P(),
            P(),
            P(),
            P(),
            P(),
            P(("shard", "dp")),
            P(("shard", "dp"), None),
            P(("shard", "dp"), None),
            P(("shard", "dp"), None),
            P(("shard", "dp"), None),
        ),
        out_specs=(P("shard", None), P("shard"), P(), P()),
        check_vma=False,
    )
```

time: 456 us -> 309 us (0.68)
  waiting for transfers between devices: 155 us -> 13.3 us
  blocking collectives: 19.6 us -> 147 us
  other arithmetic: 127 us -> 10.6 us
  Pallas kernels: 0 us -> 87.8 us
  local copies, waits for them, and re-layouts: 93.1 us -> 17.6 us
  matrix products: 25.7 us -> 0 us
    psum x2 -> x0, waiting for transfers between devices: 138 us -> none  [the longest x1 104 us: on_device(): total_hot = lax.psum(hot_grad, ('shard', 'dp'))]
    scatter-add x6 -> x0, other arithmetic: 98.7 us -> none  [the longest x2 26.4 us: on_device(): jax.ops.segment_sum(gradients[:, cold_feats:].reshape(-1, row_width), hot...]
    pallas_call x0 -> x6, Pallas kernels: none -> 87.8 us  [the longest x2 60.5 us: train(): pl.pallas_call(train_kernel, in_specs=[pl.BlockSpec(memory_space=pltpu.VM...]
    all_to_all x1 -> x4, blocking collectives: 13.7 us -> 74.6 us  [swap(): return lax.all_to_all(block, axis, split_axis=0, concat_axis=0, tiled=True)]
    all_gather x0 -> x2, blocking collectives: none -> 58.2 us  [the longest x1 47.1 us: on_device(): hot_total = lax.all_gather(hot_part, 'shard', tiled=True)]
    gather x5 -> x0, local copies, waits for them, and re-layouts: 52.5 us -> none  [the longest x2 18.2 us: on_device(): cold_vectors = fetched_rows.reshape(shards * capacity, row_width)[slot_part]]
    dot_general x12 -> x0, matrix products: 25.7 us -> none  [the longest x2 8 us: backprop(): jnp.einsum('sfe,sge->sfg', stacked, stacked, preferred_element_type=jnp.f...]
    psum x1, blocking collectives: 5.99 us -> 14 us  [on_device(): hits = lax.psum(hits.reshape(row_count), 'dp')]
  transfers between devices with their start and end apart: 5 -> 6, of which waited for: 3 -> 1; matrix products, arithmetic and copies ran while one was open for 43% -> 7% of each run, Pallas kernels for 0% -> 16%
where the time goes in v1:
time: 309 us; the launch traced here: 307 us
  blocking collectives  147 us (48%)
  Pallas kernels  87.8 us (28%)
  local copies, waits for them, and re-layouts  17.6 us (6%)
  starting transfers between devices  16.8 us (5%)
  between operations  14.4 us (5%)
  waiting for transfers between devices  13.3 us (4%)
  other arithmetic  10.6 us (3%)
    all_to_all x4, blocking collectives, swap(): return lax.all_to_all(block, axis, split_axis=0, concat_axis=0, tiled=True)  74.6 us
    pallas_call x2, Pallas kernels, train(): pl.pallas_call(train_kernel, in_specs=[pl.BlockSpec(memory_space=pltpu.VM...  60.5 us
    all_gather x1, blocking collectives, on_device(): hot_total = lax.all_gather(hot_part, 'shard', tiled=True)  47.1 us
    pallas_call x2, Pallas kernels, owner_gather(): pl.pallas_call(owner_gather_kernel, grid=(count // tile,), in_specs=[pl.B...  17.4 us
    all_to_all x4, starting transfers between devices, swap(): return lax.all_to_all(block, axis, split_axis=0, concat_axis=0, tiled=True)  16.7 us
    psum x1, blocking collectives, on_device(): hits = lax.psum(hits.reshape(row_count), 'dp')  14 us
    all_to_all x4, waiting for transfers between devices, swap(): return lax.all_to_all(block, axis, split_axis=0, concat_axis=0, tiled=True)  13.3 us
    unnamed x34, local copies, waits for them, and re-layouts  11.1 us
  transfers between devices with their start and end apart: 6, of which 1 were waited for; matrix products, arithmetic and copies ran while one was open for 7% of the time, Pallas kernels for 16%

profile of v1, /device:TPU:0, one launch (start us, length us, event | category | flops | bytes accessed | tf_op | source)
XLA Modules:
  0.0 307.4 jit_solution(11003176142989131614)
XLA Ops:
  7.2 0.9 copy.48
  8.1 0.8 fusion
  8.9 13.7 %all_to_all.45 = s32[8,1,512]{2,1,0:T(1,128)S(1)} all-to-all(s32[8,1,512]{2,1,0:T(1,128)S(1)} %all_to_all.36), channel_id=1, replica_groups=mesh['shard'=8,'dp'=4] {'shard'}, dimensions={0} | all-to-all | bytes 32768 | tf_op jit(solution)/shard_map/all_to_all | solution.py:276
  22.7 1.3 copy.52.ids_ref
  24.0 8.7 %shard_map.165 = (bf16[2048,256]{1,0:T(8,128)(2,1)}, f32[1,2048]{1,0:T(1,128)S(1)}) custom-call(s32[2048,1]{1,0:T(8,128)} %copy.52.ids_ref, bf16[2048,256]{1,0:T(8,128)(2,1)} %table_ref.3), custom_call_target="tpu_custom_call" | custom-call | flops 2147483648 | bytes 2097152 | tf_op jit(solution)/shard_map/pallas_call | solution.py:44
  32.7 3.7 %all-to-all-start.1 = ((bf16[8,256,256]{2,1,0:T(8,128)(2,1)}), bf16[8,256,256]{2,1,0:T(8,128)(2,1)S(1)}, u32[]{:S(2)}, u32[]{:S(2)}) async-start(bf16[8,256,256]{2,1,0:T(8,128)(2,1)} %bitcast.4), calls=%async_computation.1 | async-start | bytes 2097152 | tf_op jit(solution)/shard_map/all_to_all | solution.py:276
  36.4 1.4 copy.64
  37.8 1.3 copy.57.ids_ref
  39.2 8.7 %shard_map.167 = (bf16[2048,256]{1,0:T(8,128)(2,1)}, f32[1,2048]{1,0:T(1,128)S(1)}) custom-call(s32[2048,1]{1,0:T(8,128)} %copy.57.ids_ref, bf16[2048,256]{1,0:T(8,128)(2,1)} %table_ref.3), custom_call_target="tpu_custom_call" | custom-call | flops 2147483648 | bytes 2097152 | tf_op jit(solution)/shard_map/pallas_call | solution.py:44
  47.8 13.3 %all-to-all-done.1 = bf16[8,256,256]{2,1,0:T(8,128)(2,1)S(1)} async-done(((bf16[8,256,256]{2,1,0:T(8,128)(2,1)}), bf16[8,256,256]{2,1,0:T(8,128)(2,1)S(1)}, u32[]{:S(2)}, u32[]{:S(2)}) %all-to-all-start.1) | async-done | bytes 1048608 | tf_op jit(solution)/shard_map/all_to_all | solution.py:276
  61.1 1.0 copy-done.6
  62.1 4.6 %all-to-all-start.3 = ((bf16[8,256,256]{2,1,0:T(8,128)(2,1)}), bf16[8,256,256]{2,1,0:T(8,128)(2,1)}, u32[]{:S(2)}, u32[]{:S(2)}) async-start(bf16[8,256,256]{2,1,0:T(8,128)(2,1)} %bitcast.19), calls=%async_computation.3 | async-start | bytes 2097152 | tf_op jit(solution)/shard_map/all_to_all | solution.py:276
  66.7 1.4 copy.67
  68.1 1.3 convert_element_type.3.hot_ref
  69.4 0.2 copy.53
  69.6 0.1 copy.56.targets_ref
  69.8 1.3 copy.70
  71.1 1.3 copy.73
  72.5 0.1 copy.60.targets_ref
  72.6 1.1 broadcast_in_dim.11.hot_before_ref
  73.7 30.2 %shard_map.166 = (bf16[2048,256]{1,0:T(8,128)(2,1)}, f32[1024,256]{1,0:T(8,128)}) custom-call(bf16[2048,256]{1,0:T(8,128)(2,1)} %bitcast.76, s32[2048,1]{1,0:T(8,128)} %bitcast.77, s32[1,2048]{1,0:T(1,128)S(1)} %bitcast.62, s32[2048,1]{1,0:T(8,128)} %bitcast.80, s32[1,2048]{1,0:T(1,128)S(1)} %bitcast.68, bf16[1024,256]{1,0:T(8,128)(2,1)S(1)} %convert_element_type.3.hot_ref, ...), custom_call_target="tpu_custom_call" | custom-call | flops 15032385536 | bytes 12582912 | tf_op jit(solution)/shard_map/pallas_call | solution.py:224
  104.0 30.3 %shard_map.168 = (bf16[2048,256]{1,0:T(8,128)(2,1)}, f32[1024,256]{1,0:T(8,128)}) custom-call(bf16[2048,256]{1,0:T(8,128)(2,1)} %bitcast.20.fetched_ref, s32[2048,1]{1,0:T(8,128)} %bitcast.78, s32[1,2048]{1,0:T(1,128)S(1)} %bitcast.64, s32[2048,1]{1,0:T(8,128)} %bitcast.79, s32[1,2048]{1,0:T(1,128)S(1)} %bitcast.66, ...), custom_call_target="tpu_custom_call" | custom-call | flops 15032385536 | bytes 12582912 | tf_op jit(solution)/shard_map/pallas_call | solution.py:224
  134.3 17.9 %all_to_all.46 = f32[4,256,256]{2,1,0:T(8,128)S(1)} all-to-all(f32[4,256,256]{2,1,0:T(8,128)} %bitcast.82), channel_id=1, replica_groups=mesh['shard'=8,'dp'=4] {'dp'}, dimensions={0} | all-to-all | bytes 2097152 | tf_op jit(solution)/shard_map/all_to_all | solution.py:276
  152.2 0.1 reduce_sum.27
  152.3 14.1 %all_to_all.47 = f32[8,32,256]{2,1,0:T(8,128)S(1)} all-to-all(f32[8,32,256]{2,1,0:T(8,128)S(1)} %bitcast.74), channel_id=1, replica_groups=mesh['shard'=8,'dp'=4] {'shard'}, dimensions={0} | all-to-all | bytes 524288 | tf_op jit(solution)/shard_map/all_to_all | solution.py:276
  166.3 28.9 %all_to_all.48 = bf16[8,256,256]{2,1,0:T(8,128)(2,1)S(1)} all-to-all(bf16[8,256,256]{2,1,0:T(8,128)(2,1)} %bitcast.81), channel_id=1, replica_groups=mesh['shard'=8,'dp'=4] {'shard'}, dimensions={0} | all-to-all | bytes 2097152 | tf_op jit(solution)/shard_map/all_to_all | solution.py:276
  195.3 4.3 %all-to-all-start.2 = ((bf16[8,256,256]{2,1,0:T(8,128)(2,1)}), bf16[8,256,256]{2,1,0:T(8,128)(2,1)}, u32[]{:S(2)}, u32[]{:S(2)}) async-start(bf16[8,256,256]{2,1,0:T(8,128)(2,1)} %bitcast.75), calls=%async_computation.2 | async-start | bytes 2097152 | tf_op jit(solution)/shard_map/all_to_all | solution.py:276
  199.5 0.0 all-gather.6.cloned.1.call-start
  199.6 47.1 %all_gather.14 = f32[256,256]{1,0:T(8,128)} all-gather(f32[32,256]{1,0:T(8,128)S(1)} %reduce_sum.28), channel_id=1, replica_groups=mesh['shard'=8,'dp'=4] {'shard'}, dimensions={0}, use_global_device_ids=true | all-gather | bytes 294912 | tf_op jit(solution)/shard_map/all_gather | solution.py:363
  246.8 2.7 pad_maximum_fusion.grad_ref
  249.5 8.0 %shard_map.169 = bf16[2048,256]{1,0:T(8,128)(2,1)} custom-call(s32[1,4096]{1,0:T(1,128)S(1)} %reshape.107.ids_ref, bf16[4096,256]{1,0:T(8,128)(2,1)} %pad_maximum_fusion.grad_ref), custom_call_target="tpu_custom_call" | custom-call | flops 4294967296 | bytes 3145728 | tf_op jit(solution)/shard_map/pallas_call | solution.py:78
  257.5 4.2 %all-to-all-start.5 = ((bf16[4,512,256]{2,1,0:T(8,128)(2,1)}), bf16[4,512,256]{2,1,0:T(8,128)(2,1)}, u32[]{:S(2)}, u32[]{:S(2)}) async-start(bf16[4,512,256]{2,1,0:T(8,128)(2,1)} %bitcast.27), calls=%async_computation.5 | async-start | bytes 2097152 | tf_op jit(solution)/shard_map/all_to_all | solution.py:276
  261.8 0.0 all-gather.4.cloned.1.call-start
  261.8 0.8 dynamic_slice.14
  262.6 0.1 copy.62.accum_ref
  262.8 1.0 constant_dynamic-slice_fusion.1.table_ref
  263.8 14.0 %psum.7 = f32[2048]{0:T(1024)S(1)} all-reduce(f32[2048]{0:T(1024)S(1)} %bitcast.86), channel_id=1, replica_groups=mesh['shard'=8,'dp'=4] {'dp'}, use_global_device_ids=true, to_apply=%region_0.1 | all-reduce | flops 2048 | bytes 16384 | tf_op jit(solution)/shard_map/psum | solution.py:318
  277.9 0.1 dynamic_slice.12
  277.9 0.1 copy.61.hits_ref
  278.1 1.9 shard_map.170
  280.0 0.7 copy-done.1
  280.7 0.7 copy-done.3
  281.4 11.1 %all-gather = f32[2048,1]{1,0:T(8,128)S(1)} all-gather(f32[512,1]{1,0:T(8,128)} %copy-done.1), channel_id=2, replica_groups=mesh['shard'=8,'dp'=4] {'dp'}, dimensions={0}, use_global_device_ids=true | all-gather | bytes 10240 | tf_op jit(solution)/shard_map/all_gather | solution.py:358
  292.5 0.9 reduce.1
  293.5 1.4 multiply_reduce_fusion
  294.9 0.6 fusion.1
  295.5 2.7 divide_subtract_fusion
  298.3 2.3 copy.77
  (42 shorter events, 0.3 us)
Async XLA Ops:
  7.2 256.6 %copy-start = (s32[2048,256]{1,0:T(8,128)S(1)}, s32[2048,256]{1,0:T(8,128)}, u32[]{:S(2)}) copy-start(s32[2048,256]{1,0:T(8,128)} %param.16) | copy-start | bytes 6291460
  32.7 3.7 %copy-start.7 = (s32[512,8]{0,1:T(8,128)S(1)}, s32[512,8]{0,1:T(8,128)}, u32[]{:S(2)}) copy-start(s32[512,8]{0,1:T(8,128)} %param.25) | copy-start | bytes 49156
  32.7 28.4 %all-to-all-start.1 = ((bf16[8,256,256]{2,1,0:T(8,128)(2,1)}), bf16[8,256,256]{2,1,0:T(8,128)(2,1)S(1)}, u32[]{:S(2)}, u32[]{:S(2)}) async-start(bf16[8,256,256]{2,1,0:T(8,128)(2,1)} %bitcast.4), calls=%async_computation.1 | async-start | bytes 2097152 | tf_op jit(solution)/shard_map/all_to_all | solution.py:276
  47.8 18.9 %copy-start.8 = (s32[512,8]{0,1:T(8,128)S(1)}, s32[512,8]{0,1:T(8,128)}, u32[]{:S(2)}) copy-start(s32[512,8]{0,1:T(8,128)} %param.24) | copy-start | bytes 49156
  61.1 1.0 copy-start.6
  62.1 7.3 %copy-start.2 = (bf16[256,512]{1,0:T(8,128)(2,1)S(1)}, bf16[256,512]{1,0:T(8,128)(2,1)}, u32[]{:S(2)}) copy-start(bf16[256,512]{1,0:T(8,128)(2,1)} %w_inter_ref.3) | copy-start | bytes 786436
  62.1 41.8 %all-to-all-start.3 = ((bf16[8,256,256]{2,1,0:T(8,128)(2,1)}), bf16[8,256,256]{2,1,0:T(8,128)(2,1)}, u32[]{:S(2)}, u32[]{:S(2)}) async-start(bf16[8,256,256]{2,1,0:T(8,128)(2,1)} %bitcast.19), calls=%async_computation.3 | async-start | bytes 2097152 | tf_op jit(solution)/shard_map/all_to_all | solution.py:276
  66.7 2.9 copy-start.10
  69.4 4.3 %copy-start.4 = (f32[512]{0:T(512)S(1)}, f32[512]{0:T(512)}, u32[]{:S(2)}) copy-start(f32[512]{0:T(512)} %param.21) | copy-start | bytes 6148
  69.4 4.3 %copy-start.5 = (f32[512]{0:T(512)S(1)}, f32[512]{0:T(512)}, u32[]{:S(2)}) copy-start(f32[512]{0:T(512)} %param.22) | copy-start | bytes 6148
  195.3 51.5 %all-to-all-start.2 = ((bf16[8,256,256]{2,1,0:T(8,128)(2,1)}), bf16[8,256,256]{2,1,0:T(8,128)(2,1)}, u32[]{:S(2)}, u32[]{:S(2)}) async-start(bf16[8,256,256]{2,1,0:T(8,128)(2,1)} %bitcast.75), calls=%async_computation.2 | async-start | bytes 2097152 | tf_op jit(solution)/shard_map/all_to_all | solution.py:276
  199.5 94.0 %all-gather.6.cloned.1.call-start = ((), (), s32[]{:S(2)}) async-start(), calls=%async_computation.9 | async-start | bytes 1310720 | tf_op jit(solution)/shard_map/all_gather | solution.py:364
  257.5 20.6 %all-to-all-start.5 = ((bf16[4,512,256]{2,1,0:T(8,128)(2,1)}), bf16[4,512,256]{2,1,0:T(8,128)(2,1)}, u32[]{:S(2)}, u32[]{:S(2)}) async-start(bf16[4,512,256]{2,1,0:T(8,128)(2,1)} %bitcast.27), calls=%async_computation.5 | async-start | bytes 2097152 | tf_op jit(solution)/shard_map/all_to_all | solution.py:276
  261.8 36.5 %all-gather.4.cloned.1.call-start = ((), (), s32[]{:S(2)}) async-start(), calls=%async_computation.8 | async-start | bytes 1310720 | tf_op jit(solution)/shard_map/all_gather | solution.py:357
  280.0 0.7 copy-start.1
  280.7 0.7 copy-start.3
  281.4 13.5 %copy-start.9 = (f32[1024]{0:T(1024)S(1)}, f32[1024]{0:T(1024)}, u32[]{:S(2)}) copy-start(f32[1024]{0:T(1024)} %param.18) | copy-start | bytes 12292
Sparse Core Ops, SparseCore 0:
  246.9 15.4 all-gather.5
  281.6 16.4 all-gather.3

commit v2 on v1

--- a/solution.py
+++ b/solution.py
@@ -63,34 +63,6 @@
             transcendentals=0,
         ),
     )(ids, table)
-
-
-def owner_scatter_kernel(ids_ref, grad_ref, out_ref):
-    tile = out_ref.shape[0]
-    count = ids_ref.shape[1]
-    pick = hot_one(tile, count, ids_ref[...], 0, pl.program_id(0) * tile)
-    out_ref[...] = dot(pick.astype(BF), grad_ref[...]).astype(out_ref.dtype)
-
-
-def owner_scatter(ids, grads, rows):
-    count, width = grads.shape
-    tile = min(256, rows)
-    return pl.pallas_call(
-        owner_scatter_kernel,
-        grid=(rows // tile,),
-        in_specs=[
-            pl.BlockSpec((1, count), lambda i: (0, 0)),
-            pl.BlockSpec((count, width), lambda i: (0, 0)),
-        ],
-        out_specs=pl.BlockSpec((tile, width), lambda i: (i, 0)),
-        out_shape=jax.ShapeDtypeStruct((rows, width), BF),
-        compiler_params=pltpu.CompilerParams(vmem_limit_bytes=VMEM_LIMIT),
-        cost_estimate=pl.CostEstimate(
-            flops=2 * count * rows * width,
-            bytes_accessed=2 * (count + rows) * width,
-            transcendentals=0,
-        ),
-    )(ids, grads)
 
 
 def train_kernel(
@@ -245,31 +217,273 @@
     )(*operands)
 
 
-def cold_update_kernel(parts_ref, hits_ref, table_ref, accum_ref, bits_ref, out_ref, accum_out_ref):
-    grad = parts_ref[0].astype(F32)
-    for d in range(1, parts_ref.shape[0]):
-        grad = grad + parts_ref[d].astype(F32)
-    hits = hits_ref[...]
+def to_column(row):
+    return jnp.transpose(jnp.broadcast_to(row, (8, row.shape[1])))[:, :1]
+
+
+def to_row(column):
+    return jnp.transpose(jnp.broadcast_to(column, (column.shape[0], 128)))[:1, :]
+
+
+def tail_kernel(
+    shards,
+    copies,
+    micros,
+    ids_ref,
+    hits_ref,
+    table_ref,
+    accum_ref,
+    bits_ref,
+    hot_grad_ref,
+    hot_table_ref,
+    hot_accum_ref,
+    *rest,
+):
+    slot_refs = rest[:micros]
+    cold_out_ref, accum_out_ref, hot_out_ref, hot_accum_out_ref = rest[micros : micros + 4]
+    (
+        grads_ref,
+        parts_ref,
+        gathered_ref,
+        hits_in_ref,
+        dp_in_ref,
+        quarter_ref,
+        shard_in_ref,
+        total_ref,
+        cold_send,
+        cold_recv,
+        hits_send,
+        hits_recv,
+        dp_send,
+        dp_recv,
+        shard_send,
+        shard_recv,
+        spread_send,
+        spread_recv,
+        wide_send,
+        wide_recv,
+        part_send,
+        part_recv,
+        out_send,
+        out_recv,
+        accum_send,
+        accum_recv,
+    ) = rest[micros + 4 :]
+    s = lax.axis_index("shard")
+    d = lax.axis_index("dp")
+    share, width = parts_ref.shape[1:]
+
+    def along_shard(k):
+        return lax.rem(s + k, shards)
+
+    def along_dp(k):
+        return lax.rem(d + k, copies)
+
+    barrier = pltpu.get_barrier_semaphore()
+    for k in range(1, shards):
+        pl.semaphore_signal(
+            barrier, inc=1, device_id=(along_shard(k), d), device_id_type=pl.DeviceIdType.MESH
+        )
+    for k in range(1, copies):
+        pl.semaphore_signal(
+            barrier, inc=1, device_id=(s, along_dp(k)), device_id_type=pl.DeviceIdType.MESH
+        )
+    pl.semaphore_wait(barrier, shards + copies - 2)
+
+    def send(src, dst, send_sem, recv_sem, device):
+        copy = pltpu.make_async_remote_copy(
+            src_ref=src,
+            dst_ref=dst,
+            send_sem=send_sem,
+            recv_sem=recv_sem,
+            device_id=device,
+            device_id_type=pl.DeviceIdType.MESH,
+        )
+        copy.start()
+        return copy
+
+    def to_dp(k, src, dst, sends, receives):
+        return send(src, dst, sends.at[k - 1], receives.at[k - 1], (s, along_dp(k)))
+
+    def to_shard(k, src, dst, sends, receives, at=0):
+        j = at * (shards - 1) + k - 1
+        return send(src, dst, sends.at[j], receives.at[j], (along_shard(k), d))
+
+    hot_first = [
+        to_dp(k, hot_grad_ref.at[along_dp(k)], dp_in_ref.at[d], dp_send, dp_recv)
+        for k in range(1, copies)
+    ]
+    hit_copies = [
+        to_dp(k, hits_ref.at[along_dp(k)], hits_in_ref.at[d], hits_send, hits_recv)
+        for k in range(1, copies)
+    ]
+    cold_copies = [
+        to_shard(k, slot_refs[m].at[along_shard(k)], grads_ref.at[m, s], cold_send, cold_recv, m)
+        for m in range(micros)
+        for k in range(1, shards)
+    ]
+    for m in range(micros):
+        grads_ref[m, s] = slot_refs[m][s]
+
+    for copy in hot_first:
+        copy.wait_recv()
+    quarter_ref[...] = hot_grad_ref[d]
+    for k in range(1, copies):
+        quarter_ref[...] += dp_in_ref[along_dp(k)]
+    hot_second = [
+        to_shard(k, quarter_ref.at[along_shard(k)], shard_in_ref.at[s], shard_send, shard_recv)
+        for k in range(1, shards)
+    ]
+    for copy in hot_second:
+        copy.wait_recv()
+    total = quarter_ref[s]
+    for k in range(1, shards):
+        total = total + shard_in_ref[along_shard(k)]
+    total_ref[d, s] = total
+    hot_third = [
+        to_shard(k, total_ref.at[d, s], total_ref.at[d, s], spread_send, spread_recv)
+        for k in range(1, shards)
+    ]
+    for copy in hot_third:
+        copy.wait_recv()
+    hot_fourth = [
+        to_dp(k, total_ref.at[d], total_ref.at[d], wide_send, wide_recv) for k in range(1, copies)
+    ]
+
+    for copy in cold_copies:
+        copy.wait_recv()
+    tile = min(256, share)
+
+    def scatter(q):
+        def step(t, carry):
+            at = pl.multiple_of(t * tile, tile)
+            pick = hot_one(tile, ids_ref.shape[1], ids_ref[...], 0, q * share + at).astype(BF)
+            grads = grads_ref[...].reshape(-1, width)
+            parts_ref[q, pl.ds(at, tile), :] = dot(pick, grads).astype(BF)
+            return carry
+
+        lax.fori_loop(0, share // tile, step, 0)
+
+    part_copies = []
+    for k in range(1, copies):
+        q = along_dp(k)
+        scatter(q)
+        part_copies.append(to_dp(k, parts_ref.at[q], gathered_ref.at[d], part_send, part_recv))
+    scatter(d)
+
+    for copy in hit_copies + part_copies:
+        copy.wait_recv()
+    grad = parts_ref[d].astype(F32)
+    hits = hits_ref[d]
+    for k in range(1, copies):
+        grad = grad + gathered_ref[along_dp(k)].astype(F32)
+        hits = hits + hits_in_ref[along_dp(k)]
+    own = pl.ds(pl.multiple_of(d * share, share), share)
+    hits = to_column(hits)
     averaged = grad / jnp.maximum(hits, 1.0)
-    accum = accum_ref[...] + jnp.mean(averaged * averaged, axis=-1, keepdims=True)
-    updated = table_ref[...].astype(F32) - learn_rate * averaged / jnp.sqrt(accum)
+    accum = to_column(accum_ref[d]) + jnp.mean(averaged * averaged, axis=-1, keepdims=True)
+    accum_out_ref[d] = to_row(accum)
+    accum_copies = [
+        to_dp(k, accum_out_ref.at[d], accum_out_ref.at[d], accum_send, accum_recv)
+        for k in range(1, copies)
+    ]
+    updated = table_ref[own, :].astype(F32) - learn_rate * averaged / jnp.sqrt(accum)
     step = jnp.max(jnp.abs(updated), axis=-1, keepdims=True) / 8.0
-    dither = bits_ref[...].astype(F32) * (1.0 / 65280.0) - 0.5
-    out_ref[...] = jnp.where(hits > 0.5, updated + step * dither, updated).astype(BF)
-    accum_out_ref[...] = accum
-
-
-def cold_update(parts, hits, table, accum, bits):
-    return pl.pallas_call(
-        cold_update_kernel,
-        in_specs=[pl.BlockSpec(memory_space=pltpu.VMEM)] * 5,
-        out_specs=[pl.BlockSpec(memory_space=pltpu.VMEM)] * 2,
+    dither = bits_ref[own, :].astype(F32) * (1.0 / 65280.0) - 0.5
+    cold_out_ref[d] = jnp.where(hits > 0.5, updated + step * dither, updated).astype(BF)
+    out_copies = [
+        to_dp(k, cold_out_ref.at[d], cold_out_ref.at[d], out_send, out_recv)
+        for k in range(1, copies)
+    ]
+
+    for copy in hot_fourth:
+        copy.wait_recv()
+    hot_sum = total_ref[...].reshape(hot_table_ref.shape)
+    hot_accum = to_column(hot_accum_ref[...]) + jnp.mean(hot_sum * hot_sum, axis=-1, keepdims=True)
+    hot_out_ref[...] = hot_table_ref[...] - learn_rate * hot_sum / jnp.sqrt(hot_accum)
+    hot_accum_out_ref[...] = to_row(hot_accum)
+
+    for copy in accum_copies + out_copies:
+        copy.wait_recv()
+    for group in (hot_first, hit_copies, cold_copies, hot_second, hot_third, hot_fourth):
+        for copy in group:
+            copy.wait_send()
+    for copy in part_copies + accum_copies + out_copies:
+        copy.wait_send()
+
+
+def tail(ids, hits, table, accum, bits, hot_grad, hot_table, hot_accum, slot_grads):
+    shards = lax.axis_size("shard")
+    copies = lax.axis_size("dp")
+    micros = len(slot_grads)
+    rows, width = table.shape
+    share = rows // copies
+    hot_count = hot_table.shape[0]
+    piece = hot_count // (shards * copies)
+    capacity = slot_grads[0].shape[1]
+    operands = (
+        ids,
+        hits.reshape(copies, 1, share),
+        table,
+        accum.reshape(copies, 1, share),
+        bits,
+        hot_grad.reshape(copies, shards, piece, width),
+        hot_table,
+        hot_accum.reshape(1, -1),
+        *slot_grads,
+    )
+    shard_sem = pltpu.SemaphoreType.DMA((shards - 1,))
+    cold_sem = pltpu.SemaphoreType.DMA((micros * (shards - 1),))
+    dp_sem = pltpu.SemaphoreType.DMA((copies - 1,))
+    outs = pl.pallas_call(
+        functools.partial(tail_kernel, shards, copies, micros),
+        in_specs=[pl.BlockSpec(memory_space=pltpu.VMEM)] * len(operands),
+        out_specs=[pl.BlockSpec(memory_space=pltpu.VMEM)] * 4,
         out_shape=[
-            jax.ShapeDtypeStruct(table.shape, BF),
-            jax.ShapeDtypeStruct(accum.shape, F32),
-        ],
-        compiler_params=pltpu.CompilerParams(vmem_limit_bytes=VMEM_LIMIT),
-    )(parts, hits, table, accum, bits)
+            jax.ShapeDtypeStruct((copies, share, width), BF),
+            jax.ShapeDtypeStruct((copies, 1, share), F32),
+            jax.ShapeDtypeStruct(hot_table.shape, F32),
+            jax.ShapeDtypeStruct((1, hot_count), F32),
+        ],
+        scratch_shapes=[
+            pltpu.VMEM((micros, shards, capacity, width), BF),
+            pltpu.VMEM((copies, share, width), BF),
+            pltpu.VMEM((copies, share, width), BF),
+            pltpu.VMEM((copies, 1, share), F32),
+            pltpu.VMEM((copies, shards, piece, width), F32),
+            pltpu.VMEM((shards, piece, width), F32),
+            pltpu.VMEM((shards, piece, width), F32),
+            pltpu.VMEM((copies, shards, piece, width), F32),
+            cold_sem,
+            cold_sem,
+            dp_sem,
+            dp_sem,
+            dp_sem,
+            dp_sem,
+            shard_sem,
+            shard_sem,
+            shard_sem,
+            shard_sem,
+            dp_sem,
+            dp_sem,
+            dp_sem,
+            dp_sem,
+            dp_sem,
+            dp_sem,
+            dp_sem,
+            dp_sem,
+        ],
+        compiler_params=pltpu.CompilerParams(
+            vmem_limit_bytes=VMEM_LIMIT, collective_id=1, has_side_effects=True
+        ),
+    )(*operands)
+    cold_out, accum_out, hot_out, hot_accum_out = outs
+    return (
+        cold_out.reshape(rows, width),
+        accum_out.reshape(rows),
+        hot_out,
+        hot_accum_out.reshape(hot_count),
+    )
 
 
 def swap(block, axis):
@@ -293,11 +507,9 @@
     counts,
 ):
     shards = lax.axis_size("shard")
-    copies = lax.axis_size("dp")
     micros = counts.shape[0]
     capacity = requests.shape[1]
     row_count, width = cold_table.shape
-    hot_count = hot_table.shape[0]
     samples = targets.shape[0] // micros
     feats = cold_slots.shape[1] + hot_ids.shape[1]
 
@@ -315,14 +527,13 @@
         fetched.append(
             swap(rows.reshape(shards, capacity, width), "shard").reshape(shards * capacity, width)
         )
-    hits = lax.psum(hits.reshape(row_count), "dp")
 
     turned = w_inter.reshape(feats, feats, -1).transpose(1, 0, 2).reshape(w_inter.shape)
     hot_rows = hot_table.astype(BF)
     cold_ids = cold_slots.reshape(micros, samples, -1).transpose(0, 2, 1).reshape(micros, -1)
     hot_names = hot_ids.reshape(micros, samples, -1).transpose(0, 2, 1).reshape(micros, -1)
     hot_grad = jnp.zeros(hot_table.shape, F32)
-    owner_parts = []
+    slot_grads = []
     for m in range(micros):
         slot_grad, hot_grad = train(
             fetched[m],
@@ -339,32 +550,19 @@
             targets[m * samples : (m + 1) * samples].reshape(-1, 1),
             hot_grad,
         )
-        owner_parts.append(swap(slot_grad.reshape(shards, capacity, width), "shard"))
-    owner_grad = jnp.concatenate([part.reshape(-1, width) for part in owner_parts], axis=0)
+        slot_grads.append(slot_grad.reshape(shards, capacity, width))
     owner_ids = requested.transpose(1, 0, 2).reshape(1, -1)
-    cold_grad = owner_scatter(owner_ids, owner_grad, row_count)
-
-    share = row_count // copies
-    parts = swap(cold_grad.reshape(copies, share, width), "dp")
-    first = lax.axis_index("dp") * share
-    cold_out, cold_accum_out = cold_update(
-        parts,
-        lax.dynamic_slice_in_dim(hits, first, share).reshape(-1, 1),
-        lax.dynamic_slice_in_dim(cold_table, first, share),
-        lax.dynamic_slice_in_dim(cold_accum, first, share).reshape(-1, 1),
-        lax.dynamic_slice_in_dim(dither_bits, first, share),
+    return tail(
+        owner_ids,
+        hits,
+        cold_table,
+        cold_accum,
+        dither_bits,
+        hot_grad,
+        hot_table,
+        hot_accum,
+        slot_grads,
     )
-    cold_out = lax.all_gather(cold_out, "dp", tiled=True)
-    cold_accum_out = lax.all_gather(cold_accum_out.reshape(-1), "dp", tiled=True)
-
-    hot_part = jnp.sum(swap(hot_grad.reshape(copies, hot_count // copies, width), "dp"), axis=0)
-    hot_part = hot_part.reshape(shards, -1, width)
-    hot_part = jnp.sum(swap(hot_part, "shard"), axis=0)
-    hot_total = lax.all_gather(hot_part, "shard", tiled=True)
-    hot_total = lax.all_gather(hot_total, "dp", tiled=True)
-    hot_accum_out = hot_accum + jnp.mean(hot_total * hot_total, axis=-1)
-    hot_out = hot_table - learn_rate * hot_total / jnp.sqrt(hot_accum_out)[:, None]
-    return (cold_out, cold_accum_out, hot_out, hot_accum_out)
 
 
 def solution(mesh):

time: 309 us -> 230 us (0.74)
  blocking collectives: 147 us -> 13.7 us
  Pallas kernels: 87.8 us -> 174 us
  between operations: 14.4 us -> 0.83 us
  other arithmetic: 10.6 us -> 0.9 us
  starting transfers between devices: 16.8 us -> 8.11 us
    pallas_call x2 -> x1, Pallas kernels: 9.92 us -> 96.5 us  [tail(): pl.pallas_call(functools.partial(tail_kernel, shards, copies, micros), in...]
    all_to_all x4 -> x1, blocking collectives: 74.6 us -> 13.7 us  [swap(): return lax.all_to_all(block, axis, split_axis=0, concat_axis=0, tiled=True)]
    all_gather x2 -> x0, blocking collectives: 58.2 us -> none  [the longest x1 47.1 us: on_device(): hot_total = lax.all_gather(hot_part, 'shard', tiled=True)]
    psum x1 -> x0, blocking collectives: 14 us -> none  [on_device(): hits = lax.psum(hits.reshape(row_count), 'dp')]
    all_to_all x4 -> x2, starting transfers between devices: 16.7 us -> 8.11 us  [swap(): return lax.all_to_all(block, axis, split_axis=0, concat_axis=0, tiled=True)]
    unnamed x34 -> x35, local copies, waits for them, and re-layouts: 11.1 us -> 10.7 us
    all_to_all x4 -> x2, waiting for transfers between devices: 13.3 us -> 13.2 us  [swap(): return lax.all_to_all(block, axis, split_axis=0, concat_axis=0, tiled=True)]
  transfers between devices with their start and end apart: 6 -> 2, of which waited for: 1 -> 1; matrix products, arithmetic and copies ran while one was open for 7% -> 4% of each run, Pallas kernels for 16% -> 17%
where the time goes in v2:
time: 230 us; the launch traced here: 226 us
  Pallas kernels  174 us (76%)
  local copies, waits for them, and re-layouts  15 us (7%)
  blocking collectives  13.7 us (6%)
  waiting for transfers between devices  13.2 us (6%)
  starting transfers between devices  8.11 us (4%)
    pallas_call x1, Pallas kernels, tail(): pl.pallas_call(functools.partial(tail_kernel, shards, copies, micros), in...  96.5 us
    pallas_call x2, Pallas kernels, train(): pl.pallas_call(train_kernel, in_specs=[pl.BlockSpec(memory_space=pltpu.VM...  60.3 us
    pallas_call x2, Pallas kernels, owner_gather(): pl.pallas_call(owner_gather_kernel, grid=(count // tile,), in_specs=[pl.B...  17.4 us
    all_to_all x1, blocking collectives, swap(): return lax.all_to_all(block, axis, split_axis=0, concat_axis=0, tiled=True)  13.7 us
    all_to_all x2, waiting for transfers between devices, swap(): return lax.all_to_all(block, axis, split_axis=0, concat_axis=0, tiled=True)  13.2 us
    unnamed x35, local copies, waits for them, and re-layouts  10.7 us
    all_to_all x2, starting transfers between devices, swap(): return lax.all_to_all(block, axis, split_axis=0, concat_axis=0, tiled=True)  8.11 us
  transfers between devices with their start and end apart: 2, of which 1 were waited for; matrix products, arithmetic and copies ran while one was open for 4% of the time, Pallas kernels for 17%

profile of v2, /device:TPU:0, one launch (start us, length us, event | category | flops | bytes accessed | tf_op | source)
XLA Modules:
  0.0 225.9 jit_solution(9445333755668965007)
XLA Ops:
  0.6 0.8 copy.31
  1.4 0.8 fusion
  2.2 13.7 %all_to_all.20 = s32[8,1,512]{2,1,0:T(1,128)S(1)} all-to-all(s32[8,1,512]{2,1,0:T(1,128)S(1)} %all_to_all.16), channel_id=1, replica_groups=mesh['shard'=8,'dp'=4] {'shard'}, dimensions={0} | all-to-all | bytes 32768 | tf_op jit(solution)/shard_map/all_to_all | solution.py:490
  16.0 1.3 copy.35.ids_ref
  17.3 0.0 copy-start.7
  17.3 8.7 %shard_map.165 = (bf16[2048,256]{1,0:T(8,128)(2,1)}, f32[1,2048]{1,0:T(1,128)S(1)}) custom-call(s32[2048,1]{1,0:T(8,128)} %copy.35.ids_ref, bf16[2048,256]{1,0:T(8,128)(2,1)} %table_ref.5), custom_call_target="tpu_custom_call" | custom-call | flops 2147483648 | bytes 2097152 | tf_op jit(solution)/shard_map/pallas_call | solution.py:44
  26.0 3.6 %all-to-all-start.2 = ((bf16[8,256,256]{2,1,0:T(8,128)(2,1)}), bf16[8,256,256]{2,1,0:T(8,128)(2,1)S(1)}, u32[]{:S(2)}, u32[]{:S(2)}) async-start(bf16[8,256,256]{2,1,0:T(8,128)(2,1)} %bitcast.19), calls=%async_computation.2 | async-start | bytes 2097152 | tf_op jit(solution)/shard_map/all_to_all | solution.py:490
  29.6 0.0 copy-done.7
  29.6 1.4 copy.51
  31.0 1.3 copy.36.ids_ref
  32.3 0.0 copy-start.8
  32.3 0.0 copy-start.5
  32.3 8.7 %shard_map.166 = (bf16[2048,256]{1,0:T(8,128)(2,1)}, f32[1,2048]{1,0:T(1,128)S(1)}) custom-call(s32[2048,1]{1,0:T(8,128)} %copy.36.ids_ref, bf16[2048,256]{1,0:T(8,128)(2,1)} %table_ref.5), custom_call_target="tpu_custom_call" | custom-call | flops 2147483648 | bytes 2097152 | tf_op jit(solution)/shard_map/pallas_call | solution.py:44
  41.0 0.0 copy-start
  41.0 0.0 copy-start.9
  41.1 13.2 %all-to-all-done.2 = bf16[8,256,256]{2,1,0:T(8,128)(2,1)S(1)} async-done(((bf16[8,256,256]{2,1,0:T(8,128)(2,1)}), bf16[8,256,256]{2,1,0:T(8,128)(2,1)S(1)}, u32[]{:S(2)}, u32[]{:S(2)}) %all-to-all-start.2) | async-done | bytes 1048608 | tf_op jit(solution)/shard_map/all_to_all | solution.py:490
  54.3 0.0 copy-start.6
  54.3 0.0 copy-start.3
  54.3 0.0 copy-start.4
  54.3 4.6 %all-to-all-start.1 = ((bf16[8,256,256]{2,1,0:T(8,128)(2,1)}), bf16[8,256,256]{2,1,0:T(8,128)(2,1)}, u32[]{:S(2)}, u32[]{:S(2)}) async-start(bf16[8,256,256]{2,1,0:T(8,128)(2,1)} %bitcast.7), calls=%async_computation.1 | async-start | bytes 2097152 | tf_op jit(solution)/shard_map/all_to_all | solution.py:490
  58.9 0.0 copy-done.8
  58.9 1.4 copy.54
  60.2 0.0 copy-done.5
  60.2 0.1 convert_element_type.3.hot_ref
  60.3 0.0 copy-done
  60.3 0.2 copy.37
  60.5 0.0 copy-done.9
  60.5 0.1 copy.40.targets_ref
  60.7 1.3 copy.45
  62.0 1.3 copy.48
  63.4 0.1 copy.43.targets_ref
  63.6 1.1 broadcast_in_dim.10.hot_before_ref
  64.7 0.0 copy-done.6
  64.7 0.0 copy-done.3
  64.7 0.0 copy-done.4
  64.7 30.1 %shard_map.167 = (bf16[2048,256]{1,0:T(8,128)(2,1)}, f32[1024,256]{1,0:T(8,128)}) custom-call(bf16[2048,256]{1,0:T(8,128)(2,1)} %bitcast.81, s32[2048,1]{1,0:T(8,128)} %bitcast.82, s32[1,2048]{1,0:T(1,128)S(1)} %bitcast.63, s32[2048,1]{1,0:T(8,128)} %bitcast.85, s32[1,2048]{1,0:T(1,128)S(1)} %bitcast.69, bf16[1024,256]{1,0:T(8,128)(2,1)S(1)} %convert_element_type.3.hot_ref, ...), custom_call_target="tpu_custom_call" | custom-call | flops 15032385536 | bytes 12582912 | tf_op jit(solution)/shard_map/pallas_call | solution.py:196
  94.8 0.0 all-to-all-done.1
  94.8 0.0 copy-start.1
  94.8 0.0 copy-start.2
  94.8 30.1 %shard_map.168 = (bf16[2048,256]{1,0:T(8,128)(2,1)}, f32[1024,256]{1,0:T(8,128)}) custom-call(bf16[2048,256]{1,0:T(8,128)(2,1)} %bitcast.8.fetched_ref, s32[2048,1]{1,0:T(8,128)} %bitcast.83, s32[1,2048]{1,0:T(1,128)S(1)} %bitcast.65, s32[2048,1]{1,0:T(8,128)} %bitcast.84, s32[1,2048]{1,0:T(1,128)S(1)} %bitcast.67, ...), custom_call_target="tpu_custom_call" | custom-call | flops 15032385536 | bytes 12582912 | tf_op jit(solution)/shard_map/pallas_call | solution.py:196
  125.0 0.0 copy-done.1
  125.0 0.0 copy-done.2
  125.0 96.5 %shard_map.169 = (bf16[4,512,256]{2,1,0:T(8,128)(2,1)S(1)}, f32[4,1,512]{2,1,0:T(1,128)S(1)}, f32[1024,256]{1,0:T(8,128)}, f32[1,1024]{1,0:T(1,128)S(1)}) custom-call(s32[1,4096]{1,0:T(1,128)S(1)} %reshape.100.ids_ref, f32[4,1,512]{2,1,0:T(1,128)S(1)} %bitcast.61, bf16[2048,256]{1,0:T(8,128)(2,1)} %table_ref.5, f32[4,1,512]{2,1,0:T(1,128)S(1)} %bitcast.70, ...), custom_call_target="tpu_custom_call" | custom-call | tf_op jit(solution)/shard_map/pallas_call | solution.py:438
  221.5 1.0 copy.61
  222.4 0.6 copy.62
  223.0 2.3 %copy.63 = f32[1024,256]{1,0:T(8,128)} copy(f32[1024,256]{1,0:T(8,128)} %get-tuple-element.42) | data formatting | bytes 2097152
  225.3 0.6 copy.64
  (14 shorter events, 0.2 us)
Async XLA Ops:
  17.3 12.3 %copy-start.7 = (s32[512,8]{0,1:T(8,128)S(1)}, s32[512,8]{0,1:T(8,128)}, u32[]{:S(2)}) copy-start(s32[512,8]{0,1:T(8,128)} %param.25) | copy-start | bytes 49156
  26.0 28.3 %all-to-all-start.2 = ((bf16[8,256,256]{2,1,0:T(8,128)(2,1)}), bf16[8,256,256]{2,1,0:T(8,128)(2,1)S(1)}, u32[]{:S(2)}, u32[]{:S(2)}) async-start(bf16[8,256,256]{2,1,0:T(8,128)(2,1)} %bitcast.19), calls=%async_computation.2 | async-start | bytes 2097152 | tf_op jit(solution)/shard_map/all_to_all | solution.py:490
  32.3 26.6 %copy-start.8 = (s32[512,8]{0,1:T(8,128)S(1)}, s32[512,8]{0,1:T(8,128)}, u32[]{:S(2)}) copy-start(s32[512,8]{0,1:T(8,128)} %param.24) | copy-start | bytes 49156
  32.3 27.9 %copy-start.5 = (f32[1024,256]{1,0:T(8,128)S(1)}, f32[1024,256]{1,0:T(8,128)}, u32[]{:S(2)}) copy-start(f32[1024,256]{1,0:T(8,128)} %hot_table_ref.1) | copy-start | bytes 3145732
  41.0 19.3 %copy-start = (bf16[256,512]{1,0:T(8,128)(2,1)S(1)}, bf16[256,512]{1,0:T(8,128)(2,1)}, u32[]{:S(2)}) copy-start(bf16[256,512]{1,0:T(8,128)(2,1)} %w_inter_ref.3) | copy-start | bytes 786436
  41.0 19.4 %copy-start.9 = (f32[512]{0:T(512)S(1)}, f32[512]{0:T(512)}, u32[]{:S(2)}) copy-start(f32[512]{0:T(512)} %param.23) | copy-start | bytes 6148
  54.3 10.4 %copy-start.6 = (bf16[8,256,256]{2,1,0:T(8,128)(2,1)}, bf16[8,256,256]{2,1,0:T(8,128)(2,1)S(1)}, u32[]{:S(2)}) copy-start(bf16[8,256,256]{2,1,0:T(8,128)(2,1)S(1)} %all-to-all-done.2) | copy-start | bytes 3145732
  54.3 10.4 %copy-start.3 = (f32[512]{0:T(512)S(1)}, f32[512]{0:T(512)}, u32[]{:S(2)}) copy-start(f32[512]{0:T(512)} %param.21) | copy-start | bytes 6148
  54.3 10.4 %copy-start.4 = (f32[512]{0:T(512)S(1)}, f32[512]{0:T(512)}, u32[]{:S(2)}) copy-start(f32[512]{0:T(512)} %param.22) | copy-start | bytes 6148
  54.3 40.5 %all-to-all-start.1 = ((bf16[8,256,256]{2,1,0:T(8,128)(2,1)}), bf16[8,256,256]{2,1,0:T(8,128)(2,1)}, u32[]{:S(2)}, u32[]{:S(2)}) async-start(bf16[8,256,256]{2,1,0:T(8,128)(2,1)} %bitcast.7), calls=%async_computation.1 | async-start | bytes 2097152 | tf_op jit(solution)/shard_map/all_to_all | solution.py:490
  94.8 30.1 %copy-start.1 = (f32[2048]{0:T(1024)S(1)}, f32[2048]{0:T(1024)}, u32[]{:S(2)}) copy-start(f32[2048]{0:T(1024)} %param.15) | copy-start | bytes 24580
  94.8 30.1 %copy-start.2 = (f32[1024]{0:T(1024)S(1)}, f32[1024]{0:T(1024)}, u32[]{:S(2)}) copy-start(f32[1024]{0:T(1024)} %param.18) | copy-start | bytes 12292

commit v3 on v2

--- a/solution.py
+++ b/solution.py
@@ -24,45 +24,6 @@
 def hot_one(rows, columns, ids, axis, first):
     spots = lax.broadcasted_iota(jnp.int32, (rows, columns), axis) + first
     return jnp.where(spots == ids, 1.0, 0.0)
-
-
-def owner_gather_kernel(ids_ref, table_ref, rows_ref, hits_ref):
-    rows = table_ref.shape[0]
-    pick = hot_one(ids_ref.shape[0], rows, ids_ref[...], 1, 0)
-    rows_ref[...] = dot(pick.astype(BF), table_ref[...]).astype(BF)
-
-    @pl.when(pl.program_id(0) == 0)
-    def _():
-        hits_ref[...] = jnp.zeros_like(hits_ref)
-
-    hits_ref[...] += jnp.sum(pick, axis=0, keepdims=True)
-
-
-def owner_gather(ids, table):
-    count, (rows, width) = ids.shape[0], table.shape
-    tile = min(256, count)
-    return pl.pallas_call(
-        owner_gather_kernel,
-        grid=(count // tile,),
-        in_specs=[
-            pl.BlockSpec((tile, 1), lambda i: (i, 0)),
-            pl.BlockSpec((rows, width), lambda i: (0, 0)),
-        ],
-        out_specs=[
-            pl.BlockSpec((tile, width), lambda i: (i, 0)),
-            pl.BlockSpec((1, rows), lambda i: (0, 0)),
-        ],
-        out_shape=[
-            jax.ShapeDtypeStruct((count, width), BF),
-            jax.ShapeDtypeStruct((1, rows), F32),
-        ],
-        compiler_params=pltpu.CompilerParams(vmem_limit_bytes=VMEM_LIMIT),
-        cost_estimate=pl.CostEstimate(
-            flops=2 * count * rows * width,
-            bytes_accessed=2 * (count + rows) * width,
-            transcendentals=0,
-        ),
-    )(ids, table)
 
 
 def train_kernel(
@@ -89,7 +50,8 @@
 ):
     feats, samples, width = x_ref.shape
     cold = cold_col_ref.shape[0] // samples
-    slots = fetched_ref.shape[0]
+    shards, capacity = fetched_ref.shape[:2]
+    slots = shards * capacity
     hot_count = hot_ref.shape[0]
     scale = width ** (-0.5)
     group = 16
@@ -99,7 +61,7 @@
     def fill_cold(f, carry):
         ids = cold_col_ref[pl.ds(pl.multiple_of(f * samples, samples), samples), :]
         pick = hot_one(samples, slots, ids, 1, 0).astype(BF)
-        x_ref[f] = dot(pick, fetched_ref[...]).astype(BF)
+        x_ref[f] = dot(pick, fetched_ref[...].reshape(slots, width)).astype(BF)
         return carry
 
     lax.fori_loop(0, cold, fill_cold, 0)
@@ -165,64 +127,154 @@
                 back - high.astype(F32)
             ).astype(BF)
 
-    tile = 256
     edge = cold * samples
+    tile = max(256, capacity)
+    owners = tile // capacity
 
     def spill_cold(c, carry):
-        first = pl.multiple_of(c * tile, tile)
-        pick = hot_one(tile, edge, cold_row_ref[...], 0, first).astype(BF)
-        slot_grad_ref[pl.ds(first, tile), :] = dot(pick, high_ref[:edge, :]).astype(BF)
+        pick = hot_one(tile, edge, cold_row_ref[...], 0, c * tile).astype(BF)
+        summed = dot(pick, high_ref[:edge, :]).astype(BF)
+        slot_grad_ref[pl.ds(c * owners, owners)] = summed.reshape(owners, capacity, width)
         return carry
 
     lax.fori_loop(0, slots // tile, spill_cold, 0)
+    tile = min(256, hot_count)
 
     def spill_hot(c, carry):
         first = pl.multiple_of(c * tile, tile)
         pick = hot_one(tile, hot_row_ref.shape[1], hot_row_ref[...], 0, first).astype(BF)
         total = dot(pick, high_ref[edge:, :]) + dot(pick, low_ref[...])
         at = pl.ds(first, tile)
-        hot_grad_ref[at, :] = hot_before_ref[at, :] + total
+        hot_grad_ref[at, :] = total if hot_before_ref is None else hot_before_ref[at, :] + total
         return carry
 
     lax.fori_loop(0, hot_count // tile, spill_hot, 0)
 
 
-def train(*operands):
-    fetched, cold_col, _, hot_col, _, hot_rows, w_flat = operands[:7]
-    samples = operands[11].shape[0]
-    slots, width = fetched.shape
-    feats = (cold_col.shape[0] + hot_col.shape[0]) // samples
-    hidden = w_flat.shape[1]
+def to_column(row):
+    return jnp.transpose(jnp.broadcast_to(row, (8, row.shape[1])))[:, :1]
+
+
+def to_row(column):
+    return jnp.transpose(jnp.broadcast_to(column, (column.shape[0], 128)))[:1, :]
+
+
+def train_scratch(feats, samples, width, hot_lookups):
+    return [
+        pltpu.VMEM((feats, samples, width), BF),
+        pltpu.VMEM((samples, feats * feats), BF),
+        pltpu.VMEM((feats, samples, width), F32),
+        pltpu.VMEM((feats * samples, width), BF),
+        pltpu.VMEM((hot_lookups, width), BF),
+    ]
+
+
+def send(src, dst, send_sem, recv_sem, device):
+    copy = pltpu.make_async_remote_copy(
+        src_ref=src,
+        dst_ref=dst,
+        send_sem=send_sem,
+        recv_sem=recv_sem,
+        device_id=device,
+        device_id_type=pl.DeviceIdType.MESH,
+    )
+    copy.start()
+    return copy
+
+
+def fetch_kernel(shards, micros, asked_ref, table_ref, *rest):
+    network = rest[:11]
+    fetched_ref, requested_ref, hits_ref, slot_grad_ref, hot_grad_ref = rest[11:16]
+    rows_ref = rest[16]
+    scratch = rest[17:22]
+    ask_send, ask_recv, row_send, row_recv = rest[22:]
+    s = lax.axis_index("shard")
+    d = lax.axis_index("dp")
+    capacity = fetched_ref.shape[2]
+    rows = table_ref.shape[0]
+
+    def along_shard(k):
+        return lax.rem(s + k, shards)
+
+    barrier = pltpu.get_barrier_semaphore()
+    for k in range(1, shards):
+        pl.semaphore_signal(
+            barrier, inc=1, device_id=(along_shard(k), d), device_id_type=pl.DeviceIdType.MESH
+        )
+    pl.semaphore_wait(barrier, shards - 1)
+
+    asks = []
+    for k in range(1, shards):
+        p = along_shard(k)
+        sems = (ask_send.at[k - 1], ask_recv.at[k - 1])
+        asks.append(send(asked_ref.at[p], requested_ref.at[s], *sems, (p, d)))
+    requested_ref[s] = asked_ref[s]
+    for copy in asks:
+        copy.wait_recv()
+
+    hits_ref[...] = jnp.zeros_like(hits_ref)
+    moves = []
+    for m in range(micros):
+        sent = []
+        for k in [*range(1, shards), 0]:
+            p = along_shard(k)
+            ids = to_column(requested_ref[p])[m * capacity : (m + 1) * capacity, :]
+            pick = hot_one(capacity, rows, ids, 1, 0)
+            hits_ref[...] += jnp.sum(pick, axis=0, keepdims=True)
+            found = dot(pick.astype(BF), table_ref[...]).astype(BF)
+            if k == 0:
+                fetched_ref[m, s] = found
+                continue
+            rows_ref[m, p] = found
+            j = m * (shards - 1) + k - 1
+            sems = (row_send.at[j], row_recv.at[j])
+            sent.append(send(rows_ref.at[m, p], fetched_ref.at[m, s], *sems, (p, d)))
+        moves.append(sent)
+
+    for copy in moves[0]:
+        copy.wait_recv()
+    train_kernel(fetched_ref.at[0], *network, None, slot_grad_ref, hot_grad_ref, *scratch)
+    for sent in moves[1:]:
+        for copy in sent:
+            copy.wait_recv()
+    for copy in asks + sum(moves, []):
+        copy.wait_send()
+
+
+def fetch(asked, table, network, micros):
+    shards, _, asked_count = asked.shape
+    capacity = asked_count // micros
+    rows, width = table.shape
+    hot_rows = network[4]
+    samples = network[-1].shape[0]
+    cold_lookups, hot_lookups = network[0].shape[0], network[2].shape[0]
+    feats = (cold_lookups + hot_lookups) // samples
+    operands = (asked, table, *network)
+    ask_sem = pltpu.SemaphoreType.DMA((shards - 1,))
+    row_sem = pltpu.SemaphoreType.DMA((micros * (shards - 1),))
     return pl.pallas_call(
-        train_kernel,
+        functools.partial(fetch_kernel, shards, micros),
         in_specs=[pl.BlockSpec(memory_space=pltpu.VMEM)] * len(operands),
-        out_specs=[pl.BlockSpec(memory_space=pltpu.VMEM)] * 2,
+        out_specs=[pl.BlockSpec(memory_space=pltpu.VMEM)] * 5,
         out_shape=[
-            jax.ShapeDtypeStruct((slots, width), BF),
+            jax.ShapeDtypeStruct((micros, shards, capacity, width), BF),
+            jax.ShapeDtypeStruct(asked.shape, jnp.int32),
+            jax.ShapeDtypeStruct((1, rows), F32),
+            jax.ShapeDtypeStruct((shards, capacity, width), BF),
             jax.ShapeDtypeStruct(hot_rows.shape, F32),
         ],
         scratch_shapes=[
-            pltpu.VMEM((feats, samples, width), BF),
-            pltpu.VMEM((samples, feats * feats), BF),
-            pltpu.VMEM((feats, samples, width), F32),
-            pltpu.VMEM((feats * samples, width), BF),
-            pltpu.VMEM((hot_col.shape[0], width), BF),
+            pltpu.VMEM((micros, shards, capacity, width), BF),
+            *train_scratch(feats, samples, width, hot_lookups),
+            ask_sem,
+            ask_sem,
+            row_sem,
+            row_sem,
         ],
-        compiler_params=pltpu.CompilerParams(vmem_limit_bytes=VMEM_LIMIT),
-        cost_estimate=pl.CostEstimate(
-            flops=4 * samples * feats * width * (hidden + slots + hot_rows.shape[0]),
-            bytes_accessed=12 * 1024 * 1024,
-            transcendentals=samples * hidden,
+        compiler_params=pltpu.CompilerParams(
+            vmem_limit_bytes=VMEM_LIMIT, collective_id=0, has_side_effects=True
         ),
     )(*operands)
-
-
-def to_column(row):
-    return jnp.transpose(jnp.broadcast_to(row, (8, row.shape[1])))[:, :1]
-
-
-def to_row(column):
-    return jnp.transpose(jnp.broadcast_to(column, (column.shape[0], 128)))[:1, :]
 
 
 def tail_kernel(
@@ -234,13 +286,18 @@
     table_ref,
     accum_ref,
     bits_ref,
-    hot_grad_ref,
+    hot_before_ref,
     hot_table_ref,
     hot_accum_ref,
+    slot_before_ref,
+    fetched_ref,
     *rest,
 ):
-    slot_refs = rest[:micros]
-    cold_out_ref, accum_out_ref, hot_out_ref, hot_accum_out_ref = rest[micros : micros + 4]
+    networks = [rest[i * 11 : i * 11 + 11] for i in range(micros - 1)]
+    rest = rest[11 * (micros - 1) :]
+    cold_out_ref, accum_out_ref, hot_out_ref, hot_accum_out_ref = rest[:4]
+    slots_ref, hot_grad_ref = rest[4:6]
+    scratch = rest[6:11]
     (
         grads_ref,
         parts_ref,
@@ -268,10 +325,11 @@
         out_recv,
         accum_send,
         accum_recv,
-    ) = rest[micros + 4 :]
+    ) = rest[11:]
     s = lax.axis_index("shard")
     d = lax.axis_index("dp")
     share, width = parts_ref.shape[1:]
+    quarter = dp_in_ref.shape[1]
 
     def along_shard(k):
         return lax.rem(s + k, shards)
@@ -290,18 +348,6 @@
         )
     pl.semaphore_wait(barrier, shards + copies - 2)
 
-    def send(src, dst, send_sem, recv_sem, device):
-        copy = pltpu.make_async_remote_copy(
-            src_ref=src,
-            dst_ref=dst,
-            send_sem=send_sem,
-            recv_sem=recv_sem,
-            device_id=device,
-            device_id_type=pl.DeviceIdType.MESH,
-        )
-        copy.start()
-        return copy
-
     def to_dp(k, src, dst, sends, receives):
         return send(src, dst, sends.at[k - 1], receives.at[k - 1], (s, along_dp(k)))
 
@@ -309,27 +355,45 @@
         j = at * (shards - 1) + k - 1
         return send(src, dst, sends.at[j], receives.at[j], (along_shard(k), d))
 
-    hot_first = [
-        to_dp(k, hot_grad_ref.at[along_dp(k)], dp_in_ref.at[d], dp_send, dp_recv)
-        for k in range(1, copies)
-    ]
     hit_copies = [
         to_dp(k, hits_ref.at[along_dp(k)], hits_in_ref.at[d], hits_send, hits_recv)
         for k in range(1, copies)
     ]
     cold_copies = [
-        to_shard(k, slot_refs[m].at[along_shard(k)], grads_ref.at[m, s], cold_send, cold_recv, m)
-        for m in range(micros)
+        to_shard(k, slot_before_ref.at[along_shard(k)], grads_ref.at[0, s], cold_send, cold_recv)
         for k in range(1, shards)
     ]
-    for m in range(micros):
-        grads_ref[m, s] = slot_refs[m][s]
+    grads_ref[0, s] = slot_before_ref[s]
+    before = hot_before_ref
+    for m in range(1, micros):
+        made_ref = slots_ref.at[m - 1]
+        train_kernel(
+            fetched_ref.at[m], *networks[m - 1], before, made_ref, hot_grad_ref, *scratch
+        )
+        before = hot_grad_ref
+        if m == micros - 1:
+            hot_first = [
+                to_dp(
+                    k,
+                    hot_grad_ref.at[pl.ds(pl.multiple_of(along_dp(k) * quarter, 8), quarter)],
+                    dp_in_ref.at[d],
+                    dp_send,
+                    dp_recv,
+                )
+                for k in range(1, copies)
+            ]
+        cold_copies += [
+            to_shard(k, made_ref.at[along_shard(k)], grads_ref.at[m, s], cold_send, cold_recv, m)
+            for k in range(1, shards)
+        ]
+        grads_ref[m, s] = made_ref[s]
 
     for copy in hot_first:
         copy.wait_recv()
-    quarter_ref[...] = hot_grad_ref[d]
+    summed = hot_grad_ref[pl.ds(pl.multiple_of(d * quarter, 8), quarter), :]
     for k in range(1, copies):
-        quarter_ref[...] += dp_in_ref[along_dp(k)]
+        summed = summed + dp_in_ref[along_dp(k)]
+    quarter_ref[...] = summed.reshape(quarter_ref.shape)
     hot_second = [
         to_shard(k, quarter_ref.at[along_shard(k)], shard_in_ref.at[s], shard_send, shard_recv)
         for k in range(1, shards)
@@ -412,25 +476,32 @@
         copy.wait_send()
 
 
-def tail(ids, hits, table, accum, bits, hot_grad, hot_table, hot_accum, slot_grads):
+def tail(
+    ids, hits, table, accum, bits, hot_grad, hot_table, hot_accum, slot_grad, fetched, networks
+):
     shards = lax.axis_size("shard")
     copies = lax.axis_size("dp")
-    micros = len(slot_grads)
+    micros = fetched.shape[0]
+    samples = networks[0][-1].shape[0]
+    hot_lookups = networks[0][2].shape[0]
+    feats = (networks[0][0].shape[0] + hot_lookups) // samples
     rows, width = table.shape
     share = rows // copies
     hot_count = hot_table.shape[0]
     piece = hot_count // (shards * copies)
-    capacity = slot_grads[0].shape[1]
+    capacity = slot_grad.shape[1]
     operands = (
         ids,
         hits.reshape(copies, 1, share),
         table,
         accum.reshape(copies, 1, share),
         bits,
-        hot_grad.reshape(copies, shards, piece, width),
+        hot_grad,
         hot_table,
         hot_accum.reshape(1, -1),
-        *slot_grads,
+        slot_grad,
+        fetched,
+        *sum(networks, ()),
     )
     shard_sem = pltpu.SemaphoreType.DMA((shards - 1,))
     cold_sem = pltpu.SemaphoreType.DMA((micros * (shards - 1),))
@@ -446,11 +517,14 @@
             jax.ShapeDtypeStruct((1, hot_count), F32),
         ],
         scratch_shapes=[
+            pltpu.VMEM((micros - 1, shards, capacity, width), BF),
+            pltpu.VMEM(hot_table.shape, F32),
+            *train_scratch(feats, samples, width, hot_lookups),
             pltpu.VMEM((micros, shards, capacity, width), BF),
             pltpu.VMEM((copies, share, width), BF),
             pltpu.VMEM((copies, share, width), BF),
             pltpu.VMEM((copies, 1, share), F32),
-            pltpu.VMEM((copies, shards, piece, width), F32),
+            pltpu.VMEM((copies, shards * piece, width), F32),
             pltpu.VMEM((shards, piece, width), F32),
             pltpu.VMEM((shards, piece, width), F32),
             pltpu.VMEM((copies, shards, piece, width), F32),
@@ -484,10 +558,6 @@
         hot_out,
         hot_accum_out.reshape(hot_count),
     )
-
-
-def swap(block, axis):
-    return lax.all_to_all(block, axis, split_axis=0, concat_axis=0, tiled=True)
 
 
 def on_device(
@@ -509,34 +579,18 @@
     shards = lax.axis_size("shard")
     micros = counts.shape[0]
     capacity = requests.shape[1]
-    row_count, width = cold_table.shape
     samples = targets.shape[0] // micros
     feats = cold_slots.shape[1] + hot_ids.shape[1]
 
     asked = requests.reshape(micros, shards, capacity)
     live = jnp.arange(capacity, dtype=jnp.int32)[None, None, :] < counts[:, :, None]
     asked = jnp.where(live, asked, -1).transpose(1, 0, 2)
-    requested = swap(asked.reshape(shards, micros * capacity), "shard")
-    requested = requested.reshape(shards, micros, capacity)
-
-    fetched = []
-    hits = jnp.zeros((1, row_count), F32)
-    for m in range(micros):
-        rows, part_hits = owner_gather(requested[:, m].reshape(-1, 1), cold_table)
-        hits = hits + part_hits
-        fetched.append(
-            swap(rows.reshape(shards, capacity, width), "shard").reshape(shards * capacity, width)
-        )
-
     turned = w_inter.reshape(feats, feats, -1).transpose(1, 0, 2).reshape(w_inter.shape)
     hot_rows = hot_table.astype(BF)
     cold_ids = cold_slots.reshape(micros, samples, -1).transpose(0, 2, 1).reshape(micros, -1)
     hot_names = hot_ids.reshape(micros, samples, -1).transpose(0, 2, 1).reshape(micros, -1)
-    hot_grad = jnp.zeros(hot_table.shape, F32)
-    slot_grads = []
-    for m in range(micros):
-        slot_grad, hot_grad = train(
-            fetched[m],
+    networks = [
+        (
             cold_ids[m].reshape(-1, 1),
             cold_ids[m].reshape(1, -1),
             hot_names[m].reshape(-1, 1),
@@ -548,10 +602,13 @@
             hidden_bias.reshape(1, -1),
             w_out.reshape(1, -1),
             targets[m * samples : (m + 1) * samples].reshape(-1, 1),
-            hot_grad,
         )
-        slot_grads.append(slot_grad.reshape(shards, capacity, width))
-    owner_ids = requested.transpose(1, 0, 2).reshape(1, -1)
+        for m in range(micros)
+    ]
+    fetched, requested, hits, slot_grad, hot_grad = fetch(
+        asked.reshape(shards, 1, -1), cold_table, networks[0], micros
+    )
+    owner_ids = requested.reshape(shards, micros, capacity).transpose(1, 0, 2).reshape(1, -1)
     return tail(
         owner_ids,
         hits,
@@ -561,7 +618,9 @@
         hot_grad,
         hot_table,
         hot_accum,
-        slot_grads,
+        slot_grad,
+        fetched,
+        networks[1:],
     )
 
 

time: 230 us -> 195 us (0.85)
  blocking collectives: 13.7 us -> 0 us
  waiting for transfers between devices: 13.2 us -> 0 us
  starting transfers between devices: 8.11 us -> 0 us
  Pallas kernels: 174 us -> 178 us
  local copies, waits for them, and re-layouts: 15 us -> 12.1 us
    pallas_call x1, Pallas kernels: 96.5 us -> 120 us  [tail(): pl.pallas_call(functools.partial(tail_kernel, shards, copies, micros), in...]
    pallas_call x4 -> x1, Pallas kernels: 77.7 us -> 58.6 us  [fetch(): pl.pallas_call(functools.partial(fetch_kernel, shards, micros), in_specs=...]
    all_to_all x1 -> x0, blocking collectives: 13.7 us -> none  [swap(): return lax.all_to_all(block, axis, split_axis=0, concat_axis=0, tiled=True)]
    all_to_all x2 -> x0, waiting for transfers between devices: 13.2 us -> none  [swap(): return lax.all_to_all(block, axis, split_axis=0, concat_axis=0, tiled=True)]
    all_to_all x2 -> x0, starting transfers between devices: 8.11 us -> none  [swap(): return lax.all_to_all(block, axis, split_axis=0, concat_axis=0, tiled=True)]
    another operation x2 -> x0, local copies, waits for them, and re-layouts: 2.69 us -> none  [on_device(): rows, part_hits = owner_gather(requested[:, m].reshape(-1, 1), cold_table)]
  transfers between devices with their start and end apart: 2 -> 0, of which waited for: 1 -> 0; matrix products, arithmetic and copies ran while one was open for 4% -> 0% of each run, Pallas kernels for 17% -> 0%
where the time goes in v3:
time: 195 us; the launch traced here: 192 us
  Pallas kernels  178 us (91%)
  local copies, waits for them, and re-layouts  12.1 us (6%)
    pallas_call x1, Pallas kernels, tail(): pl.pallas_call(functools.partial(tail_kernel, shards, copies, micros), in...  120 us
    pallas_call x1, Pallas kernels, fetch(): pl.pallas_call(functools.partial(fetch_kernel, shards, micros), in_specs=...  58.6 us
    unnamed x35, local copies, waits for them, and re-layouts  11.6 us

profile of v3, /device:TPU:0, one launch (start us, length us, event | category | flops | bytes accessed | tf_op | source)
XLA Modules:
  0.0 191.6 jit_solution(14809290249327347049)
XLA Ops:
  0.6 0.0 copy-start.5
  0.6 0.0 copy-start
  0.7 0.8 slice_bitcast_fusion.1
  1.5 0.0 copy-start.8
  1.5 0.0 copy-start.9
  1.5 0.0 copy-start.7
  1.5 0.0 copy-start.2
  1.5 0.0 copy-start.3
  1.5 1.3 copy.33
  2.9 0.7 slice_bitcast_fusion
  3.6 1.3 copy.36
  5.0 0.0 copy-done.5
  5.0 0.1 convert_element_type.3.rest_4_
  5.0 0.0 copy-done
  5.0 0.2 copy.24
  5.2 0.0 copy-done.8
  5.2 0.1 copy.27.rest_10_
  5.4 0.0 copy-done.9
  5.4 0.1 copy.22
  5.4 0.0 copy-done.7
  5.5 0.1 fusion
  5.6 0.0 copy-done.2
  5.6 0.0 copy-done.3
  5.6 58.6 %shard_map.165 = (bf16[2,8,256,256]{3,2,1,0:T(8,128)(2,1)}, s32[8,1,512]{2,1,0:T(1,128)S(1)}, f32[1,2048]{1,0:T(1,128)S(1)}, bf16[8,256,256]{2,1,0:T(8,128)(2,1)}, f32[1024,256]{1,0:T(8,128)}) custom-call(s32[8,1,512]{2,1,0:T(1,128)S(1)} %reshape.76.asked_ref, bf16[2048,256]{1,0:T(8,128)(2,1)} %table_ref.3, s32[2048,1]{1,0:T(8,128)} %bitcast.72, ...), custom_call_target="tpu_custom_call" | custom-call | tf_op jit(solution)/shard_map/pallas_call | solution.py:255
  64.2 0.0 copy-start.1
  64.2 0.0 copy-start.4
  64.3 1.3 copy.39
  65.7 1.3 copy.42
  67.0 0.1 copy.31.rest_10_
  67.1 0.0 copy-done.1
  67.2 0.0 copy-done.4
  67.2 119.9 %shard_map.166 = (bf16[4,512,256]{2,1,0:T(8,128)(2,1)}, f32[4,1,512]{2,1,0:T(1,128)S(1)}, f32[1024,256]{1,0:T(8,128)}, f32[1,1024]{1,0:T(1,128)S(1)}) custom-call(s32[1,4096]{1,0:T(1,128)S(1)} %reshape.85.ids_ref, f32[4,1,512]{2,1,0:T(1,128)S(1)} %bitcast.62, bf16[2048,256]{1,0:T(8,128)(2,1)} %table_ref.3, f32[4,1,512]{2,1,0:T(1,128)S(1)} %bitcast.61, ...), custom_call_target="tpu_custom_call" | custom-call | tf_op jit(solution)/shard_map/pallas_call | solution.py:509
  187.0 0.0 copy-start.6
  187.0 2.4 %copy.49 = bf16[2048,256]{1,0:T(8,128)(2,1)} copy(bf16[2048,256]{1,0:T(8,128)(2,1)} %bitcast.74) | data formatting | bytes 2097152
  189.4 0.6 copy.50
  190.0 0.0 copy-done.6
  190.0 1.0 copy.51
  191.0 0.6 copy.52
  (8 shorter events, 0.1 us)
Async XLA Ops:
  0.6 4.3 %copy-start.5 = (f32[1024,256]{1,0:T(8,128)S(1)}, f32[1024,256]{1,0:T(8,128)}, u32[]{:S(2)}) copy-start(f32[1024,256]{1,0:T(8,128)} %hot_table_ref.1) | copy-start | bytes 3145732
  0.6 4.4 %copy-start = (bf16[256,512]{1,0:T(8,128)(2,1)S(1)}, bf16[256,512]{1,0:T(8,128)(2,1)}, u32[]{:S(2)}) copy-start(bf16[256,512]{1,0:T(8,128)(2,1)} %rest_6_.3) | copy-start | bytes 786436
  1.5 3.7 %copy-start.8 = (f32[512]{0:T(512)S(1)}, f32[512]{0:T(512)}, u32[]{:S(2)}) copy-start(f32[512]{0:T(512)} %param.23) | copy-start | bytes 6148
  1.5 3.9 %copy-start.9 = (s32[2,8]{1,0:T(2,128)S(1)}, s32[2,8]{1,0:T(2,128)}, u32[]{:S(2)}) copy-start(s32[2,8]{1,0:T(2,128)} %param.27) | copy-start | bytes 196
  1.5 3.9 %copy-start.7 = (s32[16,256]{1,0:T(8,128)S(1)}, s32[16,256]{1,0:T(8,128)}, u32[]{:S(2)}) copy-start(s32[16,256]{1,0:T(8,128)} %param.26) | copy-start | bytes 49156
  1.5 4.0 %copy-start.2 = (f32[512]{0:T(512)S(1)}, f32[512]{0:T(512)}, u32[]{:S(2)}) copy-start(f32[512]{0:T(512)} %param.21) | copy-start | bytes 6148
  1.5 4.0 %copy-start.3 = (f32[512]{0:T(512)S(1)}, f32[512]{0:T(512)}, u32[]{:S(2)}) copy-start(f32[512]{0:T(512)} %param.22) | copy-start | bytes 6148
  64.2 3.0 %copy-start.1 = (f32[2048]{0:T(1024)S(1)}, f32[2048]{0:T(1024)}, u32[]{:S(2)}) copy-start(f32[2048]{0:T(1024)} %param.15) | copy-start | bytes 24580
  64.2 3.0 %copy-start.4 = (f32[1024]{0:T(1024)S(1)}, f32[1024]{0:T(1024)}, u32[]{:S(2)}) copy-start(f32[1024]{0:T(1024)} %param.18) | copy-start | bytes 12292
  187.0 3.0 %copy-start.6 = (f32[1024,256]{1,0:T(8,128)S(1)}, f32[1024,256]{1,0:T(8,128)}, u32[]{:S(2)}) copy-start(f32[1024,256]{1,0:T(8,128)} %get-tuple-element.34) | copy-start | bytes 3145732
